TPU v7x, 32 devices: a whole 2x2x4 slice. The times are simulated.
32 devices in a mesh: epoch: 2 (over x), tile: 16 (over z, y, core).
Axes of the slice: x: 2, y: 2, z: 4, core: 2. Of those that a mesh axis runs over, the one named last changes fastest.
Arguments:
- owners: int32 [2, 2048], P('epoch', 'tile'), may hold values from 0 to 15, as said below
- row_offsets: int32 [2, 2048], P('epoch', 'tile'), may hold values from 0 to 224
- col_offsets: int32 [2, 2048], P('epoch', 'tile'), may hold values from 0 to 4064
- samples: bfloat16 [2, 2048, 2, 256], P('epoch', 'tile'), may hold values from -6 to 6
- coords: float32 [2, 2048, 2, 256], P('epoch', 'tile'), may hold values from 4 to 28
- taper_rows: float32 [16, 256], P('epoch'), may hold values from 1 to 4
- taper_cols: float32 [4096], P('tile'), may hold values from 1 to 4
Outputs:
- image: float32 [16, 256, 4096], P('epoch', None, 'tile')
Inputs may be any that keep to these rules, and one draw needn't show every extreme that they name: `owners`: in every epoch, within each aligned block of 128 slots (the slots of one index of tile), no owner tile is named more than 10 times, and one owner tile is named exactly 10 times in every block of that epoch.
All inputs are finite; a program needn't handle non-finite values.
Results may differ from a plain program's by a relative error of at most 0.0053.
Values may be sent and summed in bfloat16 or wider, within the bound.
A program may use at most 128 MiB of HBM per device.

v0:
```python
import functools
import math

import jax
import jax.numpy as jnp
import numpy as np
from jax import lax
from jax.experimental import pallas as pl
from jax.experimental.pallas import tpu as pltpu
from jax.sharding import PartitionSpec as P

SUB = 32
LANES = 128
VMEM_BYTES = 56 * 1024 * 1024


def kernel_weights(distance):
    return jnp.square(jnp.maximum(1.0 - jnp.square(distance * 0.25), 0.0))


def fourier(values):
    count = len(values)
    if count == 1:
        return values
    if count == 2:
        (ar, ai), (br, bi) = values
        return [(ar + br, ai + bi), (ar - br, ai - bi)]
    even, odd = fourier(values[0::2]), fourier(values[1::2])
    low, high = [], []
    for k in range(count // 2):
        (er, ei), (orr, oi) = even[k], odd[k]
        if k == 0:
            tr, ti = orr, oi
        elif 4 * k == count:
            tr, ti = -oi, orr
        elif 8 * k == count:
            s = math.sqrt(0.5)
            tr, ti = (orr - oi) * s, (orr + oi) * s
        elif 8 * k == 3 * count:
            s = math.sqrt(0.5)
            tr, ti = (orr + oi) * -s, (orr - oi) * s
        else:
            c, s = math.cos(2 * math.pi * k / count), math.sin(2 * math.pi * k / count)
            tr, ti = orr * c - oi * s, orr * s + oi * c
        low.append((er + tr, ei + ti))
        high.append((er - tr, ei - ti))
    return low + high


def grid_kernel(pairs, src_ref, data_ref, info_ref, out_ref):
    cells = lax.broadcasted_iota(jnp.int32, (SUB, data_ref.shape[2]), 0).astype(jnp.float32)

    def one(slot):
        data = data_ref[slot]
        along_u = kernel_weights(cells - data[0:1]).astype(jnp.bfloat16)
        along_v = kernel_weights(cells - data[1:2])
        weighted = jnp.concatenate([data[2:3] * along_v, data[3:4] * along_v], 0)
        return lax.dot_general(
            along_u,
            weighted.astype(jnp.bfloat16),
            (((1,), (1,)), ((), ())),
            preferred_element_type=jnp.float32,
        )

    def per_tile(tile, carry):
        for k in range(pairs):
            at = (tile * pairs + k) * 2
            both = jnp.concatenate([one(src_ref[at]), one(src_ref[at + 1])], 1)
            out_ref[tile, k * SUB : (k + 1) * SUB, :] = both.astype(jnp.bfloat16)
        out_ref[tile, pairs * SUB :, :] = info_ref[tile]
        return carry

    lax.fori_loop(0, out_ref.shape[0], per_tile, 0)


def place_kernel(
    pairs, tile_count, row_ref, block_ref, start_ref, weight_ref, pool_ref, cos_ref, sin_ref, out_ref, acc
):
    lane_blocks, acc_rows = acc.shape[1], acc.shape[2]
    rows_out = out_ref.shape[1]
    block_len = out_ref.shape[2] // 2

    def clear(i, carry):
        acc[0, i] = jnp.zeros((acc_rows, LANES), jnp.float32)
        acc[1, i] = jnp.zeros((acc_rows, LANES), jnp.float32)
        return carry

    lax.fori_loop(0, lane_blocks, clear, 0)
    shape = (SUB, 2 * LANES)
    steps = lax.broadcasted_iota(jnp.int32, shape, 1) - lax.broadcasted_iota(jnp.int32, shape, 0)

    def per_source(g, carry):
        windows = []
        weight = weight_ref[g]
        for k in range(pairs):
            block = pool_ref[g, k * SUB : (k + 1) * SUB, :]
            for j in range(2):
                start = start_ref[(g * pairs + k) * 2 + j]
                select = jnp.where(steps == start, 1.0, 0.0).astype(jnp.bfloat16)
                parts = jnp.concatenate(
                    [block[:, (2 * j + p) * SUB : (2 * j + p + 1) * SUB] for p in range(2)], 0
                )
                windows.append(jnp.dot(parts, select, preferred_element_type=jnp.float32) * weight)
        for i, window in enumerate(windows):
            at = g * pairs * 2 + i
            row, lane_block = row_ref[at], block_ref[at]
            for p in range(2):
                for h in range(2):
                    acc[p, lane_block + h, pl.ds(row, SUB), :] += window[
                        p * SUB : (p + 1) * SUB, h * LANES : (h + 1) * LANES
                    ]
        return carry

    lax.fori_loop(0, pool_ref.shape[0], per_source, 0)

    group = min(16, rows_out)
    width = min(LANES, block_len)

    def per_group(i, carry):
        for h in range(block_len // width):
            values = []
            for a in range(tile_count):
                first = a * block_len + h * width
                lane = first % LANES
                rows = pl.ds(SUB + i * group, group)
                values.append(
                    tuple(acc[p, first // LANES, rows, lane : lane + width] for p in range(2))
                )
            lanes = slice(h * width, (h + 1) * width)
            for m, (re, im) in enumerate(fourier(values)):
                c, s = cos_ref[m : m + 1, lanes], sin_ref[m : m + 1, lanes]
                turned = (re * c - im * s, re * s + im * c)
                for p in range(2):
                    first = p * block_len + h * width
                    out_ref[m, pl.ds(i * group, group), first : first + width] = turned[p].astype(
                        jnp.bfloat16
                    )
        return carry

    lax.fori_loop(0, rows_out // group, per_group, 0)


def column_kernel(got_ref, second_ref, last_ref, out_ref, mid, mixed):
    tile_count, rows_here, wide = got_ref.shape
    block_len = wide // 2

    def second(t, carry):
        mid[t] = jnp.dot(got_ref[t], second_ref[...], preferred_element_type=jnp.float32)
        return carry

    lax.fori_loop(0, tile_count, second, 0)
    group = min(16, rows_here)
    width = min(LANES, block_len)

    def per_group(i, carry):
        rows = pl.ds(i * group, group)
        for h in range(block_len // width):
            values = [
                tuple(
                    mid[t, rows, p * block_len + h * width : p * block_len + (h + 1) * width]
                    for p in range(2)
                )
                for t in range(tile_count)
            ]
            for c, parts in enumerate(fourier(values)):
                for p in range(2):
                    mixed[
                        c,
                        pl.ds(p * rows_here + i * group, group),
                        h * width : (h + 1) * width,
                    ] = parts[p].astype(jnp.bfloat16)
        return carry

    lax.fori_loop(0, rows_here // group, per_group, 0)

    def last(c, carry):
        out_ref[c] = jnp.dot(
            last_ref[c], mixed[c], preferred_element_type=jnp.float32
        ).astype(jnp.bfloat16)
        return carry

    lax.fori_loop(0, tile_count, last, 0)


def turns(product, modulus):
    angles = (product % modulus) * (2.0 * math.pi / modulus)
    return np.cos(angles), np.sin(angles)


def make_tables(tile_count, epoch_count, block_len):
    grid_size = tile_count * block_len
    long_idx = np.arange(block_len)
    tile_idx = np.arange(tile_count)
    turn_cos, turn_sin = turns(tile_idx[:, None] * long_idx[None, :], grid_size)
    c, s = turns(long_idx[:, None] * long_idx[None, :], block_len)
    second = np.concatenate([np.concatenate([c, s], 1), np.concatenate([-s, c], 1)], 0)
    rows_here = block_len // epoch_count
    row = np.arange(block_len).reshape(epoch_count, 1, 1, rows_here)
    pixel = (long_idx[None, :] * tile_count + tile_idx[:, None])[None, :, :, None]
    c, s = turns(row * pixel, grid_size)
    last = np.concatenate([c, -s], -1)
    return (
        turn_cos.astype(np.float32),
        turn_sin.astype(np.float32),
        second.astype(jnp.bfloat16),
        last.astype(jnp.bfloat16),
    )


def vmem(count):
    return [pl.BlockSpec(memory_space=pltpu.VMEM)] * count


def smem(count):
    return [pl.BlockSpec(memory_space=pltpu.SMEM)] * count


def body(tables, owners, row_offsets, col_offsets, samples, coords, taper_rows, taper_cols):
    tile_count = lax.axis_size("tile")
    epoch_count = lax.axis_size("epoch")
    epoch_index = lax.axis_index("epoch")
    slot_owner = owners[0]
    n_slots = slot_owner.shape[0]
    pairs = (max(2, n_slots * 5 // (4 * tile_count)) + 1) // 2
    capacity = 2 * pairs
    info_rows = -(-capacity // 16) * 16
    block_rows = pairs * SUB + info_rows
    block_len = taper_cols.shape[0]
    rows_here = block_len // epoch_count
    params = pltpu.CompilerParams(vmem_limit_bytes=VMEM_BYTES)
    turn_cos, turn_sin, second, last = tables

    slot_idx = jnp.arange(n_slots, dtype=jnp.int32)
    same_before = (slot_owner[:, None] == slot_owner[None, :]) & (
        slot_idx[None, :] < slot_idx[:, None]
    )
    slot_rank = jnp.sum(same_before.astype(jnp.int32), 1)
    hit = (slot_owner[None, None, :] == jnp.arange(tile_count, dtype=jnp.int32)[:, None, None]) & (
        slot_rank[None, None, :] == jnp.arange(info_rows, dtype=jnp.int32)[None, :, None]
    )
    fields = [
        jnp.sum(jnp.where(hit, f, 0), 2)
        for f in (
            jnp.ones_like(slot_owner),
            row_offsets[0],
            col_offsets[0] // LANES,
            col_offsets[0] % LANES,
            slot_idx,
        )
    ]
    source = fields[4][:, :capacity].reshape(-1)
    info = jnp.pad(jnp.stack(fields[:4], -1), ((0, 0), (0, 0), (0, LANES - 4))).astype(jnp.bfloat16)
    data = jnp.concatenate([coords[0], samples[0].astype(jnp.float32)], 1)

    packed = pl.pallas_call(
        functools.partial(grid_kernel, pairs),
        out_shape=jax.ShapeDtypeStruct((tile_count, block_rows, LANES), jnp.bfloat16),
        in_specs=smem(1) + vmem(2),
        out_specs=vmem(1)[0],
        compiler_params=params,
        name="grid_slots",
    )(source, data, info)

    got = lax.all_to_all(packed, "tile", split_axis=0, concat_axis=0, tiled=True)
    pool = [got]
    for k in range(1, epoch_count):
        ring = [(e, (e + k) % epoch_count) for e in range(epoch_count)]
        pool.append(lax.ppermute(got, "epoch", ring))
    pool = jnp.concatenate(pool, 0) if epoch_count > 1 else got
    table = pool[:, pairs * SUB : pairs * SUB + capacity, :4].astype(jnp.int32)
    valid = table[:, :, 0] > 0
    counts = jnp.sum(valid.reshape(epoch_count, -1).astype(jnp.float32), 1)
    weight = jnp.repeat(1.0 / jnp.maximum(counts, 1.0), tile_count)
    first_row = table[:, :, 1] - epoch_index * rows_here + SUB
    inside = valid & (first_row > 0) & (first_row < rows_here + SUB)
    spare = rows_here + 2 * SUB
    place_row = jnp.where(inside, first_row, spare).reshape(-1)

    sent = pl.pallas_call(
        functools.partial(place_kernel, pairs, tile_count),
        out_shape=jax.ShapeDtypeStruct((tile_count, rows_here, 2 * block_len), jnp.bfloat16),
        in_specs=smem(4) + vmem(3),
        out_specs=vmem(1)[0],
        scratch_shapes=[
            pltpu.VMEM((2, tile_count * block_len // LANES + 1, spare + SUB, LANES), jnp.float32)
        ],
        compiler_params=params,
        name="place_subgrids",
    )(
        place_row,
        table[:, :, 2].reshape(-1),
        table[:, :, 3].reshape(-1),
        weight,
        pool,
        jnp.asarray(turn_cos),
        jnp.asarray(turn_sin),
    )

    gathered = lax.all_to_all(sent, "tile", split_axis=0, concat_axis=0, tiled=True)
    last_here = lax.dynamic_index_in_dim(jnp.asarray(last), epoch_index, 0, keepdims=False)
    partial_image = pl.pallas_call(
        column_kernel,
        out_shape=jax.ShapeDtypeStruct((tile_count, block_len, block_len), jnp.bfloat16),
        in_specs=vmem(3),
        out_specs=vmem(1)[0],
        scratch_shapes=[
            pltpu.VMEM((tile_count, rows_here, 2 * block_len), jnp.float32),
            pltpu.VMEM((tile_count, 2 * rows_here, block_len), jnp.bfloat16),
        ],
        compiler_params=params,
        name="column_sections",
    )(gathered, jnp.asarray(second), last_here)

    kept = tile_count // epoch_count

    def share(k):
        to = (epoch_index + k) % epoch_count
        return lax.dynamic_slice_in_dim(partial_image, to * kept, kept, 0)

    image_sum = share(0).astype(jnp.float32)
    for k in range(1, epoch_count):
        ring = [(e, (e + k) % epoch_count) for e in range(epoch_count)]
        image_sum = image_sum + lax.ppermute(share(k), "epoch", ring).astype(jnp.float32)
    image_scale = math.sqrt(n_slots) / (64.0 * tile_count * math.sqrt(epoch_count))
    return image_sum * (image_scale * taper_rows)[:, :, None] * taper_cols[None, None, :]


def solution(mesh):
    placed = (
        P("epoch", "tile"),
        P("epoch", "tile"),
        P("epoch", "tile"),
        P("epoch", "tile", None, None),
        P("epoch", "tile", None, None),
        P("epoch", None),
        P("tile"),
    )

    def whole(owners, row_offsets, col_offsets, samples, coords, taper_rows, taper_cols):
        tables = make_tables(
            mesh.shape["tile"], mesh.shape["epoch"], taper_cols.shape[0] // mesh.shape["tile"]
        )
        return jax.shard_map(
            functools.partial(body, tables),
            mesh=mesh,
            in_specs=placed,
            out_specs=P("epoch", None, "tile"),
            check_vma=False,
        )(owners, row_offsets, col_offsets, samples, coords, taper_rows, taper_cols)

    return whole
```

profile of v0, /device:TPU:12, one launch (start us, length us, event | category | flops | bytes accessed | tf_op | source)
XLA Modules:
  0.0 175.0 jit_solution(15504269488184793644)
XLA Ops:
  0.0 0.9 convert_reduce_fusion.1
  0.9 0.7 iota_compare_fusion.2
  1.6 0.7 and_select_fusion.7
  2.3 2.1 %fusion.3 = (s32[16,16]{1,0:T(8,128)S(1)}, s32[16,16]{1,0:T(8,128)S(1)}, s32[16,16]{1,0:T(8,128)S(1)}, s32[16,16]{1,0:T(8,128)S(1)}, s32[16,16]{1,0:T(8,128)S(1)}) fusion(pred[16,128]{1,0:T(8,128)(4,1)S(1)} %iota_compare_fusion.1, pred[16,128]{1,0:T(8,128)(4,1)S(1)} %iota_compare_fusion.2, s32[128]{0:T(128)S(1)} %get-tuple-element.16, ...), kind=kLoop, calls=%fused_computation.16 | loop fusion | flops 359168 | bytes 10752 | tf_op jit(solution)/shard_map/reduce_sum | solution.py:242
  4.4 0.2 copy.17
  4.6 0.7 reshape.71.src_ref
  5.2 1.0 bitcast_convert_fusion
  6.2 0.6 pad.5.info_ref
  6.9 2.0 %pad_maximum_fusion.data_ref = f32[128,4,256]{2,1,0:T(4,128)} fusion(f32[128,2,256]{2,1,0:T(2,128)S(1)} %bitcast_convert_fusion, f32[128,2,256]{2,1,0:T(2,128)} %bitcast.32), kind=kLoop, calls=%fused_computation.2 | loop fusion | flops 131072 | bytes 1048576 | tf_op jit(solution)/shard_map/concatenate | solution.py:253
  8.9 6.6 %grid_slots.1 = bf16[16,176,128]{2,1,0:T(8,128)(2,1)} custom-call(s32[160]{0:T(256)} %reshape.71.src_ref, f32[128,4,256]{2,1,0:T(4,128)} %pad_maximum_fusion.data_ref, bf16[16,16,128]{2,1,0:T(8,128)(2,1)} %pad.5.info_ref), custom_call_target="tpu_custom_call" | custom-call | tf_op jit(solution)/shard_map/grid_slots/pallas_call | solution.py:255
  15.5 23.9 %all_to_all.10 = bf16[16,176,128]{2,1,0:T(8,128)(2,1)S(1)} all-to-all(bf16[16,176,128]{2,1,0:T(8,128)(2,1)} %grid_slots.1), channel_id=1, replica_groups=mesh['epoch'=2,'tile'=16] {'tile'}, dimensions={0} | all-to-all | bytes 1441792 | tf_op jit(solution)/shard_map/all_to_all | solution.py:264
  39.3 1.5 collective-permute-start
  40.9 16.8 %collective-permute-done = bf16[16,176,128]{2,1,0:T(8,128)(2,1)S(1)} collective-permute-done((bf16[16,176,128]{2,1,0:T(8,128)(2,1)S(1)}, bf16[16,176,128]{2,1,0:T(8,128)(2,1)S(1)}, u32[]{:S(2)}, u32[]{:S(2)}) %collective-permute-start) | collective-permute-done | bytes 720928 | tf_op jit(solution)/shard_map/ppermute | solution.py:268
  57.7 0.1 constant_dynamic-update-slice_fusion.pool_ref
  57.8 0.0 copy-start.2
  57.8 0.3 convert_reduce_fusion
  58.2 0.6 reduce.2
  58.8 0.1 gt.14
  58.9 1.9 %slice_reduce_fusion = (s32[32,10]{1,0:T(8,128)S(1)}, s32[32,10]{1,0:T(8,128)S(1)}, s32[32,10]{1,0:T(8,128)S(1)}) fusion(s32[32,10,4]{2,1,0:T(8,128)S(1)} %slice_convert_fusion, s32[]{:T(128)S(6)} %mul.31), kind=kLoop, calls=%fused_computation.8 | loop fusion | flops 640 | bytes 7684 | tf_op jit(solution)/shard_map/slice | solution.py:292
  60.8 0.1 add.45
  60.9 0.1 reduce_sum.77
  61.0 0.1 reduce_sum.78
  61.1 0.1 broadcast_in_dim.46
  61.2 0.7 reshape.72.weight_ref
  61.9 0.7 reshape_squeeze.6.block_ref
  62.6 0.7 reshape_squeeze.7.start_ref
  63.2 0.6 and_select_fusion.5.row_ref
  63.8 0.0 copy-done.2
  63.8 15.8 %place_subgrids.1 = bf16[16,128,512]{2,1,0:T(8,128)(2,1)} custom-call(s32[320]{0:T(512)} %and_select_fusion.5.row_ref, s32[320]{0:T(512)} %reshape_squeeze.6.block_ref, s32[320]{0:T(512)} %reshape_squeeze.7.start_ref, f32[32]{0:T(128)} %reshape.72.weight_ref, bf16[32,176,128]{2,1,0:T(8,128)(2,1)} %copy-done.2, f32[16,256]{1,0:T(8,128)} %constant.83.clone.cos_ref, ...), custom_call_target="tpu_custom_call" | custom-call | tf_op jit(solution)/shard_map/place_subgrids/pallas_call | solution.py:279
  79.7 5.5 %all-to-all-start.1 = ((bf16[16,128,512]{2,1,0:T(8,128)(2,1)}), bf16[16,128,512]{2,1,0:T(8,128)(2,1)S(1)}, u32[]{:S(2)}, u32[]{:S(2)}) async-start(bf16[16,128,512]{2,1,0:T(8,128)(2,1)} %place_subgrids.1), calls=%async_computation.1 | async-start | bytes 4194304 | tf_op jit(solution)/shard_map/all_to_all | solution.py:299
  85.2 3.1 %dynamic-slice_bitcast_fusion.last_ref = bf16[16,256,256]{2,1,0:T(8,128)(2,1)} fusion(bf16[2,16,256,256]{3,2,1,0:T(8,128)(2,1)} %constant.85.clone, s32[]{:T(128)S(6)} %select_n.61), kind=kLoop, calls=%fused_computation.1 | loop fusion | bytes 4194308 | tf_op jit(solution)/shard_map/jit(dynamic_index_in_dim)/squeeze | solution.py:300
  88.3 44.2 %all-to-all-done.1.got_ref = bf16[16,128,512]{2,1,0:T(8,128)(2,1)S(1)} async-done(((bf16[16,128,512]{2,1,0:T(8,128)(2,1)}), bf16[16,128,512]{2,1,0:T(8,128)(2,1)S(1)}, u32[]{:S(2)}, u32[]{:S(2)}) %all-to-all-start.1) | async-done | bytes 2097184 | tf_op jit(solution)/shard_map/all_to_all | solution.py:299
  132.5 0.0 copy-start.1
  132.5 1.3 copy-done.1
  133.8 11.6 %column_sections.1 = bf16[16,256,256]{2,1,0:T(8,128)(2,1)} custom-call(bf16[16,128,512]{2,1,0:T(8,128)(2,1)} %copy-done.1, bf16[512,512]{1,0:T(8,128)(2,1)} %constant.86.clone.second_ref, bf16[16,256,256]{2,1,0:T(8,128)(2,1)} %dynamic-slice_bitcast_fusion.last_ref), custom_call_target="tpu_custom_call" | custom-call | tf_op jit(solution)/shard_map/column_sections/pallas_call | solution.py:301
  145.3 0.0 copy-start.3
  145.3 0.0 copy-start
  145.3 0.0 copy-start.4
  145.3 2.4 %constant_dynamic-slice_fusion = bf16[8,256,256]{2,1,0:T(8,128)(2,1)} fusion(bf16[16,256,256]{2,1,0:T(8,128)(2,1)} %column_sections.1, s32[]{:T(128)S(6)} %select_n.65), kind=kLoop, calls=%fused_computation.41 | loop fusion | bytes 2097156 | tf_op jit(solution)/shard_map/dynamic_slice | solution.py:318
  147.7 1.5 collective-permute-start.1
  149.2 0.0 copy-done.3
  149.2 24.1 %collective-permute-done.1 = bf16[8,256,256]{2,1,0:T(8,128)(2,1)S(1)} collective-permute-done((bf16[8,256,256]{2,1,0:T(8,128)(2,1)}, bf16[8,256,256]{2,1,0:T(8,128)(2,1)S(1)}, u32[]{:S(2)}, u32[]{:S(2)}) %collective-permute-start.1) | collective-permute-done | bytes 1048608 | tf_op jit(solution)/shard_map/ppermute | solution.py:323
  173.3 0.0 copy-done
  173.3 0.0 copy-done.4
  173.3 1.7 multiply_multiply_fusion
  (8 shorter events, 0.1 us)
Async XLA Ops:
  39.3 18.3 %collective-permute-start = (bf16[16,176,128]{2,1,0:T(8,128)(2,1)S(1)}, bf16[16,176,128]{2,1,0:T(8,128)(2,1)S(1)}, u32[]{:S(2)}, u32[]{:S(2)}) collective-permute-start(bf16[16,176,128]{2,1,0:T(8,128)(2,1)S(1)} %all_to_all.10), channel_id=1, source_target_pairs={{0,16},{16,0},{1,17},{17,1},{2,18},{18,2},{3,19},{19,3},{4,20},{20... | collective-permute-start | bytes 2162696 | tf_op jit(solution)/shard_map/ppermute | solution.py:268
  57.8 6.0 %copy-start.2 = (bf16[32,176,128]{2,1,0:T(8,128)(2,1)}, bf16[32,176,128]{2,1,0:T(8,128)(2,1)S(1)}, u32[]{:S(2)}) copy-start(bf16[32,176,128]{2,1,0:T(8,128)(2,1)S(1)} %constant_dynamic-update-slice_fusion.pool_ref) | copy-start | bytes 4325380
  79.7 52.8 %all-to-all-start.1 = ((bf16[16,128,512]{2,1,0:T(8,128)(2,1)}), bf16[16,128,512]{2,1,0:T(8,128)(2,1)S(1)}, u32[]{:S(2)}, u32[]{:S(2)}) async-start(bf16[16,128,512]{2,1,0:T(8,128)(2,1)} %place_subgrids.1), calls=%async_computation.1 | async-start | bytes 4194304 | tf_op jit(solution)/shard_map/all_to_all | solution.py:299
  132.5 1.3 copy-start.1
  145.3 3.9 %copy-start.3 = (f32[8,256]{1,0:T(8,128)S(1)}, f32[8,256]{1,0:T(8,128)}, u32[]{:S(2)}) copy-start(f32[8,256]{1,0:T(8,128)} %param.16) | copy-start | bytes 24580
  145.3 28.0 %copy-start = (bf16[16,256,256]{2,1,0:T(8,128)(2,1)S(1)}, bf16[16,256,256]{2,1,0:T(8,128)(2,1)}, u32[]{:S(2)}) copy-start(bf16[16,256,256]{2,1,0:T(8,128)(2,1)} %column_sections.1) | copy-start | bytes 6291460
  145.3 28.0 %copy-start.4 = (f32[256]{0:T(256)S(1)}, f32[256]{0:T(256)}, u32[]{:S(2)}) copy-start(f32[256]{0:T(256)} %param.17) | copy-start | bytes 3076
  147.7 25.6 %collective-permute-start.1 = (bf16[8,256,256]{2,1,0:T(8,128)(2,1)}, bf16[8,256,256]{2,1,0:T(8,128)(2,1)S(1)}, u32[]{:S(2)}, u32[]{:S(2)}) collective-permute-start(bf16[8,256,256]{2,1,0:T(8,128)(2,1)} %constant_dynamic-slice_fusion), channel_id=1, source_target_pairs={{0,16},{16,0},{1,17},{17,1},{2,18},{18,2},{3,19},{19,3},{4,20},{20... | collective-permute-start | bytes 3145736 | tf_op jit(solution)/shard_map/ppermute | solution.py:323
where the time goes:
time: 175 us
  waiting for transfers between devices  85 us (49%)
  Pallas kernels  34 us (19%)
  blocking collectives  23.9 us (14%)
  other arithmetic  12.6 us (7%)
  local copies, waits for them, and re-layouts  10.9 us (6%)
  starting transfers between devices  8.49 us (5%)
    all_to_all x1, waiting for transfers between devices, body(): lax.all_to_all(sent, 'tile', split_axis=0, concat_axis=0, tiled=True)  44.2 us
    ppermute x1, waiting for transfers between devices, body(): lax.ppermute(share(k), 'epoch', ring).astype(jnp.float32)  24.1 us
    all_to_all x1, blocking collectives, body(): lax.all_to_all(packed, 'tile', split_axis=0, concat_axis=0, tiled=True)  23.9 us
    ppermute x1, waiting for transfers between devices, body(): pool.append(lax.ppermute(got, 'epoch', ring))  16.8 us
    pallas_call x1, Pallas kernels, body(): pl.pallas_call(functools.partial(place_kernel, pairs, tile_count), out_sh...  15.8 us
    pallas_call x1, Pallas kernels, body(): pl.pallas_call(column_kernel, out_shape=jax.ShapeDtypeStruct((tile_count,...  11.6 us
    pallas_call x1, Pallas kernels, body(): pl.pallas_call(functools.partial(grid_kernel, pairs), out_shape=jax.Shape...  6.59 us
    all_to_all x1, starting transfers between devices, body(): lax.all_to_all(sent, 'tile', split_axis=0, concat_axis=0, tiled=True)  5.5 us
  transfers between devices with their start and end apart: 3, of which 3 were waited for; matrix products, arithmetic and copies ran while one was open for 2% of the time, Pallas kernels for 0%

commit v1 on v0

--- a/solution.py
+++ b/solution.py
@@ -73,12 +73,8 @@
     lax.fori_loop(0, out_ref.shape[0], per_tile, 0)
 
 
-def place_kernel(
-    pairs, tile_count, row_ref, block_ref, start_ref, weight_ref, pool_ref, cos_ref, sin_ref, out_ref, acc
-):
+def add_slots(pairs, row_ref, block_ref, start_ref, weight_ref, pool_ref, acc):
     lane_blocks, acc_rows = acc.shape[1], acc.shape[2]
-    rows_out = out_ref.shape[1]
-    block_len = out_ref.shape[2] // 2
 
     def clear(i, carry):
         acc[0, i] = jnp.zeros((acc_rows, LANES), jnp.float32)
@@ -113,6 +109,36 @@
 
     lax.fori_loop(0, pool_ref.shape[0], per_source, 0)
 
+
+def place_kernel(pairs, row_ref, block_ref, start_ref, weight_ref, pool_ref, band_ref, acc):
+    add_slots(pairs, row_ref, block_ref, start_ref, weight_ref, pool_ref, acc)
+    rows_out = band_ref.shape[2]
+
+    def put(i, carry):
+        for p in range(2):
+            band_ref[p, i] = acc[p, i, SUB : SUB + rows_out, :].astype(jnp.bfloat16)
+        return carry
+
+    lax.fori_loop(0, band_ref.shape[1], put, 0)
+
+
+def rows_kernel(
+    pairs,
+    row_ref,
+    block_ref,
+    start_ref,
+    weight_ref,
+    pool_ref,
+    band_ref,
+    cos_ref,
+    sin_ref,
+    second_ref,
+    *rest,
+):
+    out_refs, (acc, turned_ref) = rest[:-2], rest[-2:]
+    add_slots(pairs, row_ref, block_ref, start_ref, weight_ref, pool_ref, acc)
+    tile_count, rows_out, wide = turned_ref.shape
+    block_len = wide // 2
     group = min(16, rows_out)
     width = min(LANES, block_len)
 
@@ -121,10 +147,15 @@
             values = []
             for a in range(tile_count):
                 first = a * block_len + h * width
-                lane = first % LANES
-                rows = pl.ds(SUB + i * group, group)
+                lane, at = first % LANES, first // LANES
                 values.append(
-                    tuple(acc[p, first // LANES, rows, lane : lane + width] for p in range(2))
+                    tuple(
+                        acc[p, at, pl.ds(SUB + i * group, group), lane : lane + width]
+                        + band_ref[p, at, pl.ds(i * group, group), lane : lane + width].astype(
+                            jnp.float32
+                        )
+                        for p in range(2)
+                    )
                 )
             lanes = slice(h * width, (h + 1) * width)
             for m, (re, im) in enumerate(fourier(values)):
@@ -132,54 +163,54 @@
                 turned = (re * c - im * s, re * s + im * c)
                 for p in range(2):
                     first = p * block_len + h * width
-                    out_ref[m, pl.ds(i * group, group), first : first + width] = turned[p].astype(
-                        jnp.bfloat16
-                    )
+                    turned_ref[m, pl.ds(i * group, group), first : first + width] = turned[
+                        p
+                    ].astype(jnp.bfloat16)
         return carry
 
     lax.fori_loop(0, rows_out // group, per_group, 0)
 
-
-def column_kernel(got_ref, second_ref, last_ref, out_ref, mid, mixed):
+    def per_tile(m, carry):
+        moved = jnp.dot(turned_ref[m], second_ref[...], preferred_element_type=jnp.float32)
+        for j, out_ref in enumerate(out_refs):
+            out_ref[m] = moved[:, j * 2 * width : (j + 1) * 2 * width].astype(jnp.bfloat16)
+        return carry
+
+    lax.fori_loop(0, tile_count, per_tile, 0)
+
+
+def column_kernel(epoch_ref, got_ref, last_ref, *rest):
+    out_refs, mixed = rest[:-1], rest[-1]
     tile_count, rows_here, wide = got_ref.shape
-    block_len = wide // 2
-
-    def second(t, carry):
-        mid[t] = jnp.dot(got_ref[t], second_ref[...], preferred_element_type=jnp.float32)
-        return carry
-
-    lax.fori_loop(0, tile_count, second, 0)
+    width = wide // 2
     group = min(16, rows_here)
-    width = min(LANES, block_len)
 
     def per_group(i, carry):
-        rows = pl.ds(i * group, group)
-        for h in range(block_len // width):
-            values = [
-                tuple(
-                    mid[t, rows, p * block_len + h * width : p * block_len + (h + 1) * width]
-                    for p in range(2)
-                )
-                for t in range(tile_count)
-            ]
-            for c, parts in enumerate(fourier(values)):
-                for p in range(2):
-                    mixed[
-                        c,
-                        pl.ds(p * rows_here + i * group, group),
-                        h * width : (h + 1) * width,
-                    ] = parts[p].astype(jnp.bfloat16)
+        values = [
+            tuple(
+                got_ref[t, pl.ds(i * group, group), p * width : (p + 1) * width].astype(jnp.float32)
+                for p in range(2)
+            )
+            for t in range(tile_count)
+        ]
+        for c, parts in enumerate(fourier(values)):
+            for p in range(2):
+                mixed[c, pl.ds(p * rows_here + i * group, group), :] = parts[p].astype(jnp.bfloat16)
         return carry
 
     lax.fori_loop(0, rows_here // group, per_group, 0)
-
-    def last(c, carry):
-        out_ref[c] = jnp.dot(
-            last_ref[c], mixed[c], preferred_element_type=jnp.float32
-        ).astype(jnp.bfloat16)
-        return carry
-
-    lax.fori_loop(0, tile_count, last, 0)
+    epoch_count = len(out_refs)
+    kept = tile_count // epoch_count
+    for k, out_ref in enumerate(out_refs):
+        first = lax.rem(epoch_ref[0] + k, epoch_count) * kept
+
+        def last(c, carry, out_ref=out_ref, first=first):
+            out_ref[c] = jnp.dot(
+                last_ref[first + c], mixed[first + c], preferred_element_type=jnp.float32
+            ).astype(jnp.bfloat16)
+            return carry
+
+        lax.fori_loop(0, kept, last, 0)
 
 
 def turns(product, modulus):
@@ -193,7 +224,10 @@
     tile_idx = np.arange(tile_count)
     turn_cos, turn_sin = turns(tile_idx[:, None] * long_idx[None, :], grid_size)
     c, s = turns(long_idx[:, None] * long_idx[None, :], block_len)
-    second = np.concatenate([np.concatenate([c, s], 1), np.concatenate([-s, c], 1)], 0)
+    second = np.stack([np.stack([c, s], 1), np.stack([-s, c], 1)], 0)
+    width = min(LANES, block_len)
+    second = second.reshape(2 * block_len, 2, block_len // width, width)
+    second = second.transpose(0, 2, 1, 3).reshape(2 * block_len, 2 * block_len)
     rows_here = block_len // epoch_count
     row = np.arange(block_len).reshape(epoch_count, 1, 1, rows_here)
     pixel = (long_idx[None, :] * tile_count + tile_idx[:, None])[None, :, :, None]
@@ -262,65 +296,77 @@
     )(source, data, info)
 
     got = lax.all_to_all(packed, "tile", split_axis=0, concat_axis=0, tiled=True)
-    pool = [got]
+    others = []
     for k in range(1, epoch_count):
         ring = [(e, (e + k) % epoch_count) for e in range(epoch_count)]
-        pool.append(lax.ppermute(got, "epoch", ring))
-    pool = jnp.concatenate(pool, 0) if epoch_count > 1 else got
-    table = pool[:, pairs * SUB : pairs * SUB + capacity, :4].astype(jnp.int32)
-    valid = table[:, :, 0] > 0
-    counts = jnp.sum(valid.reshape(epoch_count, -1).astype(jnp.float32), 1)
-    weight = jnp.repeat(1.0 / jnp.maximum(counts, 1.0), tile_count)
-    first_row = table[:, :, 1] - epoch_index * rows_here + SUB
-    inside = valid & (first_row > 0) & (first_row < rows_here + SUB)
+        others.append(lax.ppermute(got, "epoch", ring))
+    others = jnp.concatenate(others, 0) if epoch_count > 2 else others[0]
     spare = rows_here + 2 * SUB
-    place_row = jnp.where(inside, first_row, spare).reshape(-1)
-
+    lane_blocks = tile_count * block_len // LANES
+
+    def places(pool):
+        table = pool[:, pairs * SUB : pairs * SUB + capacity, :4].astype(jnp.int32)
+        valid = table[:, :, 0] > 0
+        counts = jnp.sum(table[:, :, 0].reshape(-1, tile_count * capacity), 1)
+        weight = jnp.repeat(1.0 / jnp.maximum(counts, 1).astype(jnp.float32), tile_count)
+        first_row = table[:, :, 1] - epoch_index * rows_here + SUB
+        inside = valid & (first_row > 0) & (first_row < rows_here + SUB)
+        place_row = jnp.where(inside, first_row, spare).reshape(-1)
+        return place_row, table[:, :, 2].reshape(-1), table[:, :, 3].reshape(-1), weight, pool
+
+    acc = pltpu.VMEM((2, lane_blocks + 1, spare + SUB, LANES), jnp.float32)
+    band = pl.pallas_call(
+        functools.partial(place_kernel, pairs),
+        out_shape=jax.ShapeDtypeStruct((2, lane_blocks, rows_here, LANES), jnp.bfloat16),
+        in_specs=smem(4) + vmem(1),
+        out_specs=vmem(1)[0],
+        scratch_shapes=[acc],
+        compiler_params=params,
+        cost_estimate=pl.CostEstimate(flops=8 * 10**9, bytes_accessed=10**7, transcendentals=0),
+        name="place_subgrids",
+    )(*places(got))
+
+    width = min(LANES, block_len)
+    chunks = block_len // width
     sent = pl.pallas_call(
-        functools.partial(place_kernel, pairs, tile_count),
-        out_shape=jax.ShapeDtypeStruct((tile_count, rows_here, 2 * block_len), jnp.bfloat16),
-        in_specs=smem(4) + vmem(3),
-        out_specs=vmem(1)[0],
-        scratch_shapes=[
-            pltpu.VMEM((2, tile_count * block_len // LANES + 1, spare + SUB, LANES), jnp.float32)
+        functools.partial(rows_kernel, pairs),
+        out_shape=[
+            jax.ShapeDtypeStruct((tile_count, rows_here, 2 * width), jnp.bfloat16)
+            for _ in range(chunks)
         ],
+        in_specs=smem(4) + vmem(5),
+        out_specs=vmem(chunks),
+        scratch_shapes=[acc, pltpu.VMEM((tile_count, rows_here, 2 * block_len), jnp.bfloat16)],
         compiler_params=params,
-        name="place_subgrids",
-    )(
-        place_row,
-        table[:, :, 2].reshape(-1),
-        table[:, :, 3].reshape(-1),
-        weight,
-        pool,
-        jnp.asarray(turn_cos),
-        jnp.asarray(turn_sin),
-    )
-
-    gathered = lax.all_to_all(sent, "tile", split_axis=0, concat_axis=0, tiled=True)
+        name="row_sections",
+    )(*places(others), band, jnp.asarray(turn_cos), jnp.asarray(turn_sin), jnp.asarray(second))
+
     last_here = lax.dynamic_index_in_dim(jnp.asarray(last), epoch_index, 0, keepdims=False)
-    partial_image = pl.pallas_call(
-        column_kernel,
-        out_shape=jax.ShapeDtypeStruct((tile_count, block_len, block_len), jnp.bfloat16),
-        in_specs=vmem(3),
-        out_specs=vmem(1)[0],
-        scratch_shapes=[
-            pltpu.VMEM((tile_count, rows_here, 2 * block_len), jnp.float32),
-            pltpu.VMEM((tile_count, 2 * rows_here, block_len), jnp.bfloat16),
-        ],
-        compiler_params=params,
-        name="column_sections",
-    )(gathered, jnp.asarray(second), last_here)
-
     kept = tile_count // epoch_count
-
-    def share(k):
-        to = (epoch_index + k) % epoch_count
-        return lax.dynamic_slice_in_dim(partial_image, to * kept, kept, 0)
-
-    image_sum = share(0).astype(jnp.float32)
-    for k in range(1, epoch_count):
-        ring = [(e, (e + k) % epoch_count) for e in range(epoch_count)]
-        image_sum = image_sum + lax.ppermute(share(k), "epoch", ring).astype(jnp.float32)
+    sums = []
+    for chunk in sent:
+        gathered = lax.all_to_all(chunk, "tile", split_axis=0, concat_axis=0, tiled=True)
+        shares = pl.pallas_call(
+            column_kernel,
+            out_shape=[
+                jax.ShapeDtypeStruct((kept, block_len, width), jnp.bfloat16)
+                for _ in range(epoch_count)
+            ],
+            in_specs=smem(1) + vmem(2),
+            out_specs=vmem(epoch_count),
+            scratch_shapes=[pltpu.VMEM((tile_count, 2 * rows_here, width), jnp.bfloat16)],
+            compiler_params=params,
+            cost_estimate=pl.CostEstimate(
+                flops=6 * 10**9, bytes_accessed=10**7, transcendentals=0
+            ),
+            name="column_sections",
+        )(epoch_index.astype(jnp.int32).reshape(1), gathered, last_here)
+        chunk_sum = shares[0].astype(jnp.float32)
+        for k in range(1, epoch_count):
+            ring = [(e, (e + k) % epoch_count) for e in range(epoch_count)]
+            chunk_sum = chunk_sum + lax.ppermute(shares[k], "epoch", ring).astype(jnp.float32)
+        sums.append(chunk_sum)
+    image_sum = jnp.concatenate(sums, 2)
     image_scale = math.sqrt(n_slots) / (64.0 * tile_count * math.sqrt(epoch_count))
     return image_sum * (image_scale * taper_rows)[:, :, None] * taper_cols[None, None, :]
 

time: 175 us -> 167 us (0.954)
  waiting for transfers between devices: 85 us -> 51.8 us
  Pallas kernels: 34 us -> 43.1 us
  starting transfers between devices: 8.49 us -> 15.9 us
  blocking collectives: 23.9 us -> 29.9 us
    ppermute x2 -> x3, waiting for transfers between devices: 40.9 us -> 20.2 us  [the longest x2 12.7 us: body(): lax.ppermute(shares[k], 'epoch', ring).astype(jnp.float32)]
    all_to_all x1 -> x2, waiting for transfers between devices: 44.2 us -> 31.6 us  [the longest x1 17.7 us: body(): lax.all_to_all(packed, 'tile', split_axis=0, concat_axis=0, tiled=True)]
    pallas_call x2 -> x4, Pallas kernels: 27.4 us -> 36.5 us  [the longest x1 15.2 us: body(): pl.pallas_call(functools.partial(rows_kernel, pairs), out_shape=[jax.Shap...]
    all_to_all x1, blocking collectives: 23.9 us -> 29.9 us  [body(): lax.all_to_all(chunk, 'tile', split_axis=0, concat_axis=0, tiled=True)]
    all_to_all x1 -> x2, starting transfers between devices: 5.5 us -> 11.4 us  [the longest x1 6.24 us: body(): lax.all_to_all(packed, 'tile', split_axis=0, concat_axis=0, tiled=True)]
    reduce_sum x2, other arithmetic: 0.44 us -> 3.16 us  [places(): counts = jnp.sum(table[:, :, 0].reshape(-1, tile_count * capacity), 1)]
    dynamic_slice x1 -> x0, local copies, waits for them, and re-layouts: 2.41 us -> none  [share(): return lax.dynamic_slice_in_dim(partial_image, to * kept, kept, 0)]
    slice x1 -> x0, other arithmetic: 1.92 us -> none  [body(): table[:, :, 3].reshape(-1)]
  transfers between devices with their start and end apart: 3 -> 5, of which waited for: 3 -> 4; matrix products, arithmetic and copies ran while one was open for 2% -> 2% of each run, Pallas kernels for 0% -> 13%
where the time goes in v1:
time: 167 us; the launch traced here: 166 us
  waiting for transfers between devices  51.8 us (31%)
  Pallas kernels  43.1 us (26%)
  blocking collectives  29.9 us (18%)
  starting transfers between devices  15.9 us (10%)
  other arithmetic  14.2 us (9%)
  local copies, waits for them, and re-layouts  9.55 us (6%)
    all_to_all x1, blocking collectives, body(): lax.all_to_all(chunk, 'tile', split_axis=0, concat_axis=0, tiled=True)  29.9 us
    all_to_all x1, waiting for transfers between devices, body(): lax.all_to_all(packed, 'tile', split_axis=0, concat_axis=0, tiled=True)  17.7 us
    pallas_call x1, Pallas kernels, body(): pl.pallas_call(functools.partial(rows_kernel, pairs), out_shape=[jax.Shap...  15.2 us
    all_to_all x1, waiting for transfers between devices, body(): lax.all_to_all(chunk, 'tile', split_axis=0, concat_axis=0, tiled=True)  13.9 us
    ppermute x2, waiting for transfers between devices, body(): lax.ppermute(shares[k], 'epoch', ring).astype(jnp.float32)  12.7 us
    pallas_call x2, Pallas kernels, body(): pl.pallas_call(column_kernel, out_shape=[jax.ShapeDtypeStruct((kept, bloc...  12.5 us
    pallas_call x1, Pallas kernels, body(): pl.pallas_call(functools.partial(place_kernel, pairs), out_shape=jax.Shap...  8.84 us
    ppermute x1, waiting for transfers between devices, body(): others.append(lax.ppermute(got, 'epoch', ring))  7.53 us
  transfers between devices with their start and end apart: 5, of which 4 were waited for; matrix products, arithmetic and copies ran while one was open for 2% of the time, Pallas kernels for 13%

profile of v1, /device:TPU:12, one launch (start us, length us, event | category | flops | bytes accessed | tf_op | source)
XLA Modules:
  0.0 166.0 jit_solution(6434086757959689134)
XLA Ops:
  0.0 0.9 convert_reduce_fusion
  0.9 0.7 iota_compare_fusion.2
  1.6 0.7 and_select_fusion.8
  2.2 2.1 %fusion.2 = (s32[16,16]{1,0:T(8,128)S(1)}, s32[16,16]{1,0:T(8,128)S(1)}, s32[16,16]{1,0:T(8,128)S(1)}, s32[16,16]{1,0:T(8,128)S(1)}, s32[16,16]{1,0:T(8,128)S(1)}) fusion(pred[16,128]{1,0:T(8,128)(4,1)S(1)} %iota_compare_fusion.1, pred[16,128]{1,0:T(8,128)(4,1)S(1)} %iota_compare_fusion.2, s32[128]{0:T(128)S(1)} %get-tuple-element.31, ...), kind=kLoop, calls=%fused_computation.12 | loop fusion | flops 359168 | bytes 10752 | tf_op jit(solution)/shard_map/reduce_sum | solution.py:276
  4.3 0.7 reshape.101.src_ref
  5.0 0.2 copy.17
  5.2 1.0 bitcast_convert_fusion
  6.2 0.6 pad.5.info_ref
  6.9 2.0 %pad_maximum_fusion.data_ref = f32[128,4,256]{2,1,0:T(4,128)} fusion(f32[128,2,256]{2,1,0:T(2,128)S(1)} %bitcast_convert_fusion, f32[128,2,256]{2,1,0:T(2,128)} %bitcast.33), kind=kLoop, calls=%fused_computation.5 | loop fusion | flops 131072 | bytes 1048576 | tf_op jit(solution)/shard_map/concatenate | solution.py:287
  8.8 6.6 %grid_slots.1 = bf16[16,176,128]{2,1,0:T(8,128)(2,1)} custom-call(s32[160]{0:T(256)} %reshape.101.src_ref, f32[128,4,256]{2,1,0:T(4,128)} %pad_maximum_fusion.data_ref, bf16[16,16,128]{2,1,0:T(8,128)(2,1)} %pad.5.info_ref), custom_call_target="tpu_custom_call" | custom-call | tf_op jit(solution)/shard_map/grid_slots/pallas_call | solution.py:289
  15.4 6.2 %all-to-all-start = ((bf16[16,176,128]{2,1,0:T(8,128)(2,1)}), bf16[16,176,128]{2,1,0:T(8,128)(2,1)S(1)}, u32[]{:S(2)}, u32[]{:S(2)}) async-start(bf16[16,176,128]{2,1,0:T(8,128)(2,1)} %grid_slots.1), calls=%async_computation | async-start | bytes 1441792 | tf_op jit(solution)/shard_map/all_to_all | solution.py:298
  21.7 17.7 %all-to-all-done.pool_ref = bf16[16,176,128]{2,1,0:T(8,128)(2,1)S(1)} async-done(((bf16[16,176,128]{2,1,0:T(8,128)(2,1)}), bf16[16,176,128]{2,1,0:T(8,128)(2,1)S(1)}, u32[]{:S(2)}, u32[]{:S(2)}) %all-to-all-start) | async-done | bytes 720928 | tf_op jit(solution)/shard_map/all_to_all | solution.py:298
  39.4 0.0 copy-start.1
  39.4 0.4 compare_reduce_fusion
  39.7 1.6 slice_reduce_fusion.4
  42.0 0.1 gt.26
  42.1 0.7 reshape_squeeze.17.start_ref
  42.7 0.7 reshape_squeeze.16.block_ref
  43.4 0.1 add.37
  43.5 0.6 and_select_fusion.5.row_ref
  44.1 1.5 collective-permute-start
  45.6 0.5 reshape.103.weight_ref
  46.1 0.0 copy-done.1
  46.1 8.8 %place_subgrids.1.band_ref = bf16[2,32,128,128]{3,2,1,0:T(8,128)(2,1)} custom-call(s32[160]{0:T(256)} %and_select_fusion.5.row_ref, s32[160]{0:T(256)} %reshape_squeeze.16.block_ref, s32[160]{0:T(256)} %reshape_squeeze.17.start_ref, f32[16]{0:T(128)} %reshape.103.weight_ref, bf16[16,176,128]{2,1,0:T(8,128)(2,1)} %copy-done.1), custom_call_target="tpu_custom_call" | custom-call | flops 8000000000 | bytes 10000000 | tf_op jit(solution)/shard_map/place_subgrids/pallas_call | solution.py:318
  54.9 7.5 %collective-permute-done.pool_ref = bf16[16,176,128]{2,1,0:T(8,128)(2,1)S(1)} collective-permute-done((bf16[16,176,128]{2,1,0:T(8,128)(2,1)S(1)}, bf16[16,176,128]{2,1,0:T(8,128)(2,1)S(1)}, u32[]{:S(2)}, u32[]{:S(2)}) %collective-permute-start) | collective-permute-done | bytes 720928 | tf_op jit(solution)/shard_map/ppermute | solution.py:302
  62.4 0.0 copy-start.2
  62.4 0.4 compare_reduce_fusion.1
  62.8 1.6 slice_reduce_fusion.5
  65.1 0.1 gt.23
  65.2 0.6 reshape_squeeze.15.start_ref
  65.8 0.6 reshape_squeeze.14.block_ref
  66.4 0.1 add.35
  66.5 0.6 and_select_fusion.6.row_ref
  67.1 0.5 reshape.102.weight_ref
  67.6 0.0 copy-done.2
  67.6 15.2 %row_sections.1 = (bf16[16,128,256]{2,1,0:T(8,128)(2,1)}, bf16[16,128,256]{2,1,0:T(8,128)(2,1)}) custom-call(s32[160]{0:T(256)} %and_select_fusion.6.row_ref, s32[160]{0:T(256)} %reshape_squeeze.14.block_ref, s32[160]{0:T(256)} %reshape_squeeze.15.start_ref, f32[16]{0:T(128)} %reshape.102.weight_ref, bf16[16,176,128]{2,1,0:T(8,128)(2,1)} %copy-done.2, ...), custom_call_target="tpu_custom_call" | custom-call | tf_op jit(solution)/shard_map/row_sections/pallas_call | solution.py:331
  82.8 29.9 %all_to_all.15.got_ref = bf16[16,128,256]{2,1,0:T(8,128)(2,1)} all-to-all(bf16[16,128,256]{2,1,0:T(8,128)(2,1)} %get-tuple-element.14), channel_id=1, replica_groups=mesh['epoch'=2,'tile'=16] {'tile'}, dimensions={0} | all-to-all | bytes 2097152 | tf_op jit(solution)/shard_map/all_to_all | solution.py:348
  112.7 5.2 %all-to-all-start.1 = ((bf16[16,128,256]{2,1,0:T(8,128)(2,1)}), bf16[16,128,256]{2,1,0:T(8,128)(2,1)S(1)}, u32[]{:S(2)}, u32[]{:S(2)}) async-start(bf16[16,128,256]{2,1,0:T(8,128)(2,1)} %get-tuple-element.11), calls=%async_computation.1 | async-start | bytes 2097152 | tf_op jit(solution)/shard_map/all_to_all | solution.py:348
  117.9 3.1 %dynamic-slice_bitcast_fusion.last_ref = bf16[16,256,256]{2,1,0:T(8,128)(2,1)} fusion(bf16[2,16,256,256]{3,2,1,0:T(8,128)(2,1)} %constant.70.clone, s32[]{:T(128)S(6)} %select_n.50), kind=kLoop, calls=%fused_computation.2 | loop fusion | bytes 4194308 | tf_op jit(solution)/shard_map/jit(dynamic_index_in_dim)/squeeze | solution.py:344
  121.0 6.3 %column_sections.3 = (bf16[8,256,128]{2,1,0:T(8,128)(2,1)}, bf16[8,256,128]{2,1,0:T(8,128)(2,1)}) custom-call(s32[1]{0:T(128)} %bitcast.epoch_ref, bf16[16,128,256]{2,1,0:T(8,128)(2,1)} %all_to_all.15.got_ref, bf16[16,256,256]{2,1,0:T(8,128)(2,1)} %dynamic-slice_bitcast_fusion.last_ref), custom_call_target="tpu_custom_call" | custom-call | flops 6000000000 | bytes 10000000 | tf_op jit(solution)/shard_map/column_sections/pallas_call | solution.py:349
  127.2 0.0 copy-start.5
  127.2 0.0 copy-start.3
  127.3 1.5 collective-permute-start.2
  128.7 13.9 %all-to-all-done.1.got_ref = bf16[16,128,256]{2,1,0:T(8,128)(2,1)S(1)} async-done(((bf16[16,128,256]{2,1,0:T(8,128)(2,1)}), bf16[16,128,256]{2,1,0:T(8,128)(2,1)S(1)}, u32[]{:S(2)}, u32[]{:S(2)}) %all-to-all-start.1) | async-done | bytes 1048608 | tf_op jit(solution)/shard_map/all_to_all | solution.py:348
  142.6 0.0 copy-start
  142.6 1.0 copy-done
  143.6 6.2 %column_sections.2 = (bf16[8,256,128]{2,1,0:T(8,128)(2,1)}, bf16[8,256,128]{2,1,0:T(8,128)(2,1)}) custom-call(s32[1]{0:T(128)} %bitcast.epoch_ref, bf16[16,128,256]{2,1,0:T(8,128)(2,1)} %copy-done, bf16[16,256,256]{2,1,0:T(8,128)(2,1)} %dynamic-slice_bitcast_fusion.last_ref), custom_call_target="tpu_custom_call" | custom-call | flops 6000000000 | bytes 10000000 | tf_op jit(solution)/shard_map/column_sections/pallas_call | solution.py:349
  149.8 0.0 copy-start.4
  149.8 1.5 collective-permute-start.1
  151.3 0.0 copy-done.5
  151.3 0.0 collective-permute-done.2
  151.3 0.0 copy-done.3
  151.3 0.0 copy-start.6
  151.3 0.1 convert_add_fusion
  151.5 12.7 %collective-permute-done.1 = bf16[8,256,128]{2,1,0:T(8,128)(2,1)S(1)} collective-permute-done((bf16[8,256,128]{2,1,0:T(8,128)(2,1)}, bf16[8,256,128]{2,1,0:T(8,128)(2,1)S(1)}, u32[]{:S(2)}, u32[]{:S(2)}) %collective-permute-start.1) | collective-permute-done | bytes 524320 | tf_op jit(solution)/shard_map/ppermute | solution.py:367
  164.2 0.0 copy-done.4
  164.2 0.1 convert_add_fusion.1
  164.3 0.0 copy-done.6
  164.3 1.7 %fusion = f32[8,256,256]{2,1,0:T(8,128)} fusion(f32[8,256,128]{2,1,0:T(8,128)S(1)} %convert_add_fusion, f32[8,256,128]{2,1,0:T(8,128)S(1)} %convert_add_fusion.1, f32[256]{0:T(256)S(1)} %copy-done.6, f32[8,256]{1,0:T(8,128)S(1)} %broadcast_multiply_fusion), kind=kLoop, calls=%fused_computation.1 | loop fusion | flops 1572864 | bytes 4203520 | tf_op jit(solution)/shard_map/mul | solution.py:371
  (7 shorter events, 0.1 us)
Async XLA Ops:
  15.4 23.9 %all-to-all-start = ((bf16[16,176,128]{2,1,0:T(8,128)(2,1)}), bf16[16,176,128]{2,1,0:T(8,128)(2,1)S(1)}, u32[]{:S(2)}, u32[]{:S(2)}) async-start(bf16[16,176,128]{2,1,0:T(8,128)(2,1)} %grid_slots.1), calls=%async_computation | async-start | bytes 1441792 | tf_op jit(solution)/shard_map/all_to_all | solution.py:298
  39.4 6.7 %copy-start.1 = (bf16[16,176,128]{2,1,0:T(8,128)(2,1)}, bf16[16,176,128]{2,1,0:T(8,128)(2,1)S(1)}, u32[]{:S(2)}) copy-start(bf16[16,176,128]{2,1,0:T(8,128)(2,1)S(1)} %all-to-all-done.pool_ref) | copy-start | bytes 2162692
  44.1 18.3 %collective-permute-start = (bf16[16,176,128]{2,1,0:T(8,128)(2,1)S(1)}, bf16[16,176,128]{2,1,0:T(8,128)(2,1)S(1)}, u32[]{:S(2)}, u32[]{:S(2)}) collective-permute-start(bf16[16,176,128]{2,1,0:T(8,128)(2,1)S(1)} %all-to-all-done.pool_ref), channel_id=1, source_target_pairs={{0,16},{16,0},{1,17},{17,1},{2,18},{18,2},{3,19},{19,3},{4,20},{20... | collective-permute-start | bytes 2162696 | tf_op jit(solution)/shard_map/ppermute | solution.py:302
  62.4 5.2 %copy-start.2 = (bf16[16,176,128]{2,1,0:T(8,128)(2,1)}, bf16[16,176,128]{2,1,0:T(8,128)(2,1)S(1)}, u32[]{:S(2)}) copy-start(bf16[16,176,128]{2,1,0:T(8,128)(2,1)S(1)} %collective-permute-done.pool_ref) | copy-start | bytes 2162692
  112.7 29.9 %all-to-all-start.1 = ((bf16[16,128,256]{2,1,0:T(8,128)(2,1)}), bf16[16,128,256]{2,1,0:T(8,128)(2,1)S(1)}, u32[]{:S(2)}, u32[]{:S(2)}) async-start(bf16[16,128,256]{2,1,0:T(8,128)(2,1)} %get-tuple-element.11), calls=%async_computation.1 | async-start | bytes 2097152 | tf_op jit(solution)/shard_map/all_to_all | solution.py:348
  127.2 24.1 %copy-start.5 = (f32[8,256]{1,0:T(8,128)S(1)}, f32[8,256]{1,0:T(8,128)}, u32[]{:S(2)}) copy-start(f32[8,256]{1,0:T(8,128)} %param.16) | copy-start | bytes 24580
  127.2 24.1 %copy-start.3 = (bf16[8,256,128]{2,1,0:T(8,128)(2,1)S(1)}, bf16[8,256,128]{2,1,0:T(8,128)(2,1)}, u32[]{:S(2)}) copy-start(bf16[8,256,128]{2,1,0:T(8,128)(2,1)} %get-tuple-element.15) | copy-start | bytes 1572868
  127.3 24.1 %collective-permute-start.2 = (bf16[8,256,128]{2,1,0:T(8,128)(2,1)}, bf16[8,256,128]{2,1,0:T(8,128)(2,1)S(1)}, u32[]{:S(2)}, u32[]{:S(2)}) collective-permute-start(bf16[8,256,128]{2,1,0:T(8,128)(2,1)} %get-tuple-element.16), channel_id=1, source_target_pairs={{0,16},{16,0},{1,17},{17,1},{2,18},{18,2},{3,19},{19,3},{4,20},{20... | collective-permute-start | bytes 1572872 | tf_op jit(solution)/shard_map/ppermute | solution.py:367
  142.6 1.0 copy-start
  149.8 14.4 %copy-start.4 = (bf16[8,256,128]{2,1,0:T(8,128)(2,1)S(1)}, bf16[8,256,128]{2,1,0:T(8,128)(2,1)}, u32[]{:S(2)}) copy-start(bf16[8,256,128]{2,1,0:T(8,128)(2,1)} %get-tuple-element.12) | copy-start | bytes 1572868
  149.8 14.3 %collective-permute-start.1 = (bf16[8,256,128]{2,1,0:T(8,128)(2,1)}, bf16[8,256,128]{2,1,0:T(8,128)(2,1)S(1)}, u32[]{:S(2)}, u32[]{:S(2)}) collective-permute-start(bf16[8,256,128]{2,1,0:T(8,128)(2,1)} %get-tuple-element.13), channel_id=1, source_target_pairs={{0,16},{16,0},{1,17},{17,1},{2,18},{18,2},{3,19},{19,3},{4,20},{20... | collective-permute-start | bytes 1572872 | tf_op jit(solution)/shard_map/ppermute | solution.py:367
  151.3 13.0 %copy-start.6 = (f32[256]{0:T(256)S(1)}, f32[256]{0:T(256)}, u32[]{:S(2)}) copy-start(f32[256]{0:T(256)} %param.17) | copy-start | bytes 3076

commit v2 on v1

--- a/solution.py
+++ b/solution.py
@@ -179,38 +179,127 @@
     lax.fori_loop(0, tile_count, per_tile, 0)
 
 
-def column_kernel(epoch_ref, got_ref, last_ref, *rest):
-    out_refs, mixed = rest[:-1], rest[-1]
-    tile_count, rows_here, wide = got_ref.shape
-    width = wide // 2
+def columns_kernel(tile_count, epoch_count, chunks, *refs):
+    sent, last_ref, outs = refs[:chunks], refs[chunks], refs[chunks + 1 : 2 * chunks + 1]
+    got, mixed, share, landed, t_send, t_recv, x_send, x_recv, own_sem = refs[2 * chunks + 1 :]
+    rows_here, width = got.shape[2], got.shape[3] // 2
+    kept = tile_count // epoch_count
+    me, epoch = lax.axis_index("tile"), lax.axis_index("epoch")
+    mesh_id = pl.DeviceIdType.MESH
+
+    barrier = pltpu.get_barrier_semaphore()
+
+    def greet(k, carry):
+        peer = lax.rem(me + k, tile_count)
+        pl.semaphore_signal(barrier, inc=1, device_id={"tile": peer}, device_id_type=mesh_id)
+        return carry
+
+    lax.fori_loop(1, tile_count, greet, 0)
+    for k in range(1, epoch_count):
+        peer = lax.rem(epoch + k, epoch_count)
+        pl.semaphore_signal(barrier, inc=1, device_id={"epoch": peer}, device_id_type=mesh_id)
+    pl.semaphore_wait(barrier, tile_count + epoch_count - 2)
+
+    def tile_copy(j, k):
+        peer = lax.rem(me + k, tile_count)
+        return pltpu.make_async_remote_copy(
+            src_ref=sent[j].at[peer],
+            dst_ref=got.at[j, me],
+            send_sem=t_send.at[j * tile_count + k],
+            recv_sem=t_recv.at[j * tile_count + k],
+            device_id={"tile": peer},
+            device_id_type=mesh_id,
+        )
+
+    def epoch_copy(j, k, c):
+        at = (j * (epoch_count - 1) + k - 1) * kept + c
+        return pltpu.make_async_remote_copy(
+            src_ref=share.at[j, k - 1, c],
+            dst_ref=landed.at[j, k - 1, c],
+            send_sem=x_send.at[at],
+            recv_sem=x_recv.at[at],
+            device_id={"epoch": lax.rem(epoch + k, epoch_count)},
+            device_id_type=mesh_id,
+        )
+
+    def own_copy(j):
+        return pltpu.make_async_copy(sent[j].at[me], got.at[j, me], own_sem.at[j])
+
+    for j in range(chunks):
+
+        def send(k, carry, j=j):
+            tile_copy(j, k).start()
+            return carry
+
+        lax.fori_loop(1, tile_count, send, 0)
+        own_copy(j).start()
+
     group = min(16, rows_here)
-
-    def per_group(i, carry):
-        values = [
-            tuple(
-                got_ref[t, pl.ds(i * group, group), p * width : (p + 1) * width].astype(jnp.float32)
-                for p in range(2)
+    for j in range(chunks):
+
+        def receive(k, carry, j=j):
+            tile_copy(j, k).wait_recv()
+            return carry
+
+        lax.fori_loop(1, tile_count, receive, 0)
+        own_copy(j).wait()
+
+        def per_group(i, carry, j=j):
+            values = [
+                tuple(
+                    got[
+                        j, t, pl.ds(i * group, group), p * width : (p + 1) * width
+                    ].astype(jnp.float32)
+                    for p in range(2)
+                )
+                for t in range(tile_count)
+            ]
+            for c, parts in enumerate(fourier(values)):
+                for p in range(2):
+                    mixed[c, pl.ds(p * rows_here + i * group, group), :] = parts[p].astype(
+                        jnp.bfloat16
+                    )
+            return carry
+
+        lax.fori_loop(0, rows_here // group, per_group, 0)
+
+        for k in range(1, epoch_count):
+            first = lax.rem(epoch + k, epoch_count) * kept
+
+            def away(c, carry, j=j, k=k, first=first):
+                share[j, k - 1, c] = jnp.dot(
+                    last_ref[first + c], mixed[first + c], preferred_element_type=jnp.float32
+                ).astype(jnp.bfloat16)
+                epoch_copy(j, k, c).start()
+                return carry
+
+            lax.fori_loop(0, kept, away, 0)
+
+        def home(c, carry, j=j):
+            outs[j][c] = jnp.dot(
+                last_ref[epoch * kept + c],
+                mixed[epoch * kept + c],
+                preferred_element_type=jnp.float32,
             )
-            for t in range(tile_count)
-        ]
-        for c, parts in enumerate(fourier(values)):
-            for p in range(2):
-                mixed[c, pl.ds(p * rows_here + i * group, group), :] = parts[p].astype(jnp.bfloat16)
-        return carry
-
-    lax.fori_loop(0, rows_here // group, per_group, 0)
-    epoch_count = len(out_refs)
-    kept = tile_count // epoch_count
-    for k, out_ref in enumerate(out_refs):
-        first = lax.rem(epoch_ref[0] + k, epoch_count) * kept
-
-        def last(c, carry, out_ref=out_ref, first=first):
-            out_ref[c] = jnp.dot(
-                last_ref[first + c], mixed[first + c], preferred_element_type=jnp.float32
-            ).astype(jnp.bfloat16)
             return carry
 
-        lax.fori_loop(0, kept, last, 0)
+        lax.fori_loop(0, kept, home, 0)
+
+    for j in range(chunks):
+
+        def sent_all(k, carry, j=j):
+            tile_copy(j, k).wait_send()
+            return carry
+
+        lax.fori_loop(1, tile_count, sent_all, 0)
+        for k in range(1, epoch_count):
+
+            def add(c, carry, j=j, k=k):
+                epoch_copy(j, k, c).wait()
+                outs[j][c] += landed[j, k - 1, c].astype(jnp.float32)
+                return carry
+
+            lax.fori_loop(0, kept, add, 0)
 
 
 def turns(product, modulus):
@@ -343,29 +432,32 @@
 
     last_here = lax.dynamic_index_in_dim(jnp.asarray(last), epoch_index, 0, keepdims=False)
     kept = tile_count // epoch_count
-    sums = []
-    for chunk in sent:
-        gathered = lax.all_to_all(chunk, "tile", split_axis=0, concat_axis=0, tiled=True)
-        shares = pl.pallas_call(
-            column_kernel,
-            out_shape=[
-                jax.ShapeDtypeStruct((kept, block_len, width), jnp.bfloat16)
-                for _ in range(epoch_count)
-            ],
-            in_specs=smem(1) + vmem(2),
-            out_specs=vmem(epoch_count),
-            scratch_shapes=[pltpu.VMEM((tile_count, 2 * rows_here, width), jnp.bfloat16)],
-            compiler_params=params,
-            cost_estimate=pl.CostEstimate(
-                flops=6 * 10**9, bytes_accessed=10**7, transcendentals=0
-            ),
-            name="column_sections",
-        )(epoch_index.astype(jnp.int32).reshape(1), gathered, last_here)
-        chunk_sum = shares[0].astype(jnp.float32)
-        for k in range(1, epoch_count):
-            ring = [(e, (e + k) % epoch_count) for e in range(epoch_count)]
-            chunk_sum = chunk_sum + lax.ppermute(shares[k], "epoch", ring).astype(jnp.float32)
-        sums.append(chunk_sum)
+    shares_shape = (chunks, epoch_count - 1, kept, block_len, width)
+    tile_sems = pltpu.SemaphoreType.DMA((chunks * tile_count,))
+    epoch_sems = pltpu.SemaphoreType.DMA((chunks * (epoch_count - 1) * kept,))
+    sums = pl.pallas_call(
+        functools.partial(columns_kernel, tile_count, epoch_count, chunks),
+        out_shape=[
+            jax.ShapeDtypeStruct((kept, block_len, width), jnp.float32) for _ in range(chunks)
+        ],
+        in_specs=vmem(chunks + 1),
+        out_specs=vmem(chunks),
+        scratch_shapes=[
+            pltpu.VMEM((chunks, tile_count, rows_here, 2 * width), jnp.bfloat16),
+            pltpu.VMEM((tile_count, 2 * rows_here, width), jnp.bfloat16),
+            pltpu.VMEM(shares_shape, jnp.bfloat16),
+            pltpu.VMEM(shares_shape, jnp.bfloat16),
+            tile_sems,
+            tile_sems,
+            epoch_sems,
+            epoch_sems,
+            pltpu.SemaphoreType.DMA((chunks,)),
+        ],
+        compiler_params=pltpu.CompilerParams(
+            vmem_limit_bytes=VMEM_BYTES, collective_id=0, has_side_effects=True
+        ),
+        name="columns",
+    )(*sent, last_here)
     image_sum = jnp.concatenate(sums, 2)
     image_scale = math.sqrt(n_slots) / (64.0 * tile_count * math.sqrt(epoch_count))
     return image_sum * (image_scale * taper_rows)[:, :, None] * taper_cols[None, None, :]

time: 167 us -> 154 us (0.922)
  Pallas kernels: 43.1 us -> 98.1 us
  blocking collectives: 29.9 us -> 0 us
  waiting for transfers between devices: 51.8 us -> 22 us
  starting transfers between devices: 15.9 us -> 7.8 us
    pallas_call x2 -> x1, Pallas kernels: 12.5 us -> 67.5 us  [body(): pl.pallas_call(functools.partial(columns_kernel, tile_count, epoch_count,...]
    all_to_all x1 -> x0, blocking collectives: 29.9 us -> none  [body(): lax.all_to_all(chunk, 'tile', split_axis=0, concat_axis=0, tiled=True)]
    all_to_all x1 -> x0, waiting for transfers between devices: 13.9 us -> none  [body(): lax.all_to_all(chunk, 'tile', split_axis=0, concat_axis=0, tiled=True)]
    ppermute x2 -> x0, waiting for transfers between devices: 12.7 us -> none  [body(): lax.ppermute(shares[k], 'epoch', ring).astype(jnp.float32)]
    all_to_all x1 -> x0, starting transfers between devices: 5.16 us -> none  [body(): lax.all_to_all(chunk, 'tile', split_axis=0, concat_axis=0, tiled=True)]
    all_to_all x1, waiting for transfers between devices: 17.7 us -> 14.5 us  [body(): lax.all_to_all(packed, 'tile', split_axis=0, concat_axis=0, tiled=True)]
    ppermute x2 -> x0, starting transfers between devices: 2.98 us -> none  [body(): lax.ppermute(shares[k], 'epoch', ring).astype(jnp.float32)]
  transfers between devices with their start and end apart: 5 -> 2, of which waited for: 4 -> 2; matrix products, arithmetic and copies ran while one was open for 2% -> 2% of each run, Pallas kernels for 13% -> 6%
where the time goes in v2:
time: 154 us
  Pallas kernels  98.1 us (64%)
  waiting for transfers between devices  22 us (14%)
  other arithmetic  15.5 us (10%)
  local copies, waits for them, and re-layouts  8.68 us (6%)
  starting transfers between devices  7.8 us (5%)
    pallas_call x1, Pallas kernels, body(): pl.pallas_call(functools.partial(columns_kernel, tile_count, epoch_count,...  67.5 us
    pallas_call x1, Pallas kernels, body(): pl.pallas_call(functools.partial(rows_kernel, pairs), out_shape=[jax.Shap...  15.2 us
    all_to_all x1, waiting for transfers between devices, body(): lax.all_to_all(packed, 'tile', split_axis=0, concat_axis=0, tiled=True)  14.5 us
    pallas_call x1, Pallas kernels, body(): pl.pallas_call(functools.partial(place_kernel, pairs), out_shape=jax.Shap...  8.84 us
    ppermute x1, waiting for transfers between devices, body(): others.append(lax.ppermute(got, 'epoch', ring))  7.49 us
    pallas_call x1, Pallas kernels, body(): pl.pallas_call(functools.partial(grid_kernel, pairs), out_shape=jax.Shape...  6.59 us
    all_to_all x1, starting transfers between devices, body(): lax.all_to_all(packed, 'tile', split_axis=0, concat_axis=0, tiled=True)  6.24 us
    mul x1, other arithmetic, body(): image_sum * (image_scale * taper_rows)[:, :, None]  3.2 us
  transfers between devices with their start and end apart: 2, of which 2 were waited for; matrix products, arithmetic and copies ran while one was open for 2% of the time, Pallas kernels for 6%

profile of v2, /device:TPU:12, one launch (start us, length us, event | category | flops | bytes accessed | tf_op | source)
XLA Modules:
  0.0 153.6 jit_solution(8185732127395545793)
XLA Ops:
  0.0 0.9 convert_reduce_fusion
  0.9 0.7 iota_compare_fusion.2
  1.6 0.7 and_select_fusion.8
  2.3 2.1 %fusion.2 = (s32[16,16]{1,0:T(8,128)S(1)}, s32[16,16]{1,0:T(8,128)S(1)}, s32[16,16]{1,0:T(8,128)S(1)}, s32[16,16]{1,0:T(8,128)S(1)}, s32[16,16]{1,0:T(8,128)S(1)}) fusion(pred[16,128]{1,0:T(8,128)(4,1)S(1)} %iota_compare_fusion.1, pred[16,128]{1,0:T(8,128)(4,1)S(1)} %iota_compare_fusion.2, s32[128]{0:T(128)S(1)} %get-tuple-element.27, ...), kind=kLoop, calls=%fused_computation.10 | loop fusion | flops 359168 | bytes 10752 | tf_op jit(solution)/shard_map/reduce_sum | solution.py:365
  4.4 0.2 copy.17
  4.6 0.7 reshape.96.src_ref
  5.2 1.0 bitcast_convert_fusion
  6.2 0.6 pad.5.info_ref
  6.9 2.0 %pad_maximum_fusion.data_ref = f32[128,4,256]{2,1,0:T(4,128)} fusion(f32[128,2,256]{2,1,0:T(2,128)S(1)} %bitcast_convert_fusion, f32[128,2,256]{2,1,0:T(2,128)} %bitcast.32), kind=kLoop, calls=%fused_computation.3 | loop fusion | flops 131072 | bytes 1048576 | tf_op jit(solution)/shard_map/concatenate | solution.py:376
  8.9 6.6 %grid_slots.1 = bf16[16,176,128]{2,1,0:T(8,128)(2,1)} custom-call(s32[160]{0:T(256)} %reshape.96.src_ref, f32[128,4,256]{2,1,0:T(4,128)} %pad_maximum_fusion.data_ref, bf16[16,16,128]{2,1,0:T(8,128)(2,1)} %pad.5.info_ref), custom_call_target="tpu_custom_call" | custom-call | tf_op jit(solution)/shard_map/grid_slots/pallas_call | solution.py:378
  15.5 6.2 %all-to-all-start = ((bf16[16,176,128]{2,1,0:T(8,128)(2,1)}), bf16[16,176,128]{2,1,0:T(8,128)(2,1)S(1)}, u32[]{:S(2)}, u32[]{:S(2)}) async-start(bf16[16,176,128]{2,1,0:T(8,128)(2,1)} %grid_slots.1), calls=%async_computation | async-start | bytes 1441792 | tf_op jit(solution)/shard_map/all_to_all | solution.py:387
  21.7 0.0 copy-start.2
  21.7 3.1 %dynamic-slice_bitcast_fusion.refs_2_ = bf16[16,256,256]{2,1,0:T(8,128)(2,1)} fusion(bf16[2,16,256,256]{3,2,1,0:T(8,128)(2,1)} %constant.70.clone, s32[]{:T(128)S(6)} %select_n.50), kind=kLoop, calls=%fused_computation.2 | loop fusion | bytes 4194308 | tf_op jit(solution)/shard_map/jit(dynamic_index_in_dim)/squeeze | solution.py:433
  24.8 0.0 copy-done.2
  24.8 14.5 %all-to-all-done.pool_ref = bf16[16,176,128]{2,1,0:T(8,128)(2,1)S(1)} async-done(((bf16[16,176,128]{2,1,0:T(8,128)(2,1)}), bf16[16,176,128]{2,1,0:T(8,128)(2,1)S(1)}, u32[]{:S(2)}, u32[]{:S(2)}) %all-to-all-start) | async-done | bytes 720928 | tf_op jit(solution)/shard_map/all_to_all | solution.py:387
  39.4 0.0 copy-start
  39.4 0.4 compare_reduce_fusion
  39.8 1.6 %slice_reduce_fusion.4 = (s32[]{:T(128)}, s32[16,10]{1,0:T(8,128)S(1)}, s32[16,10]{1,0:T(8,128)S(1)}, s32[16,10]{1,0:T(8,128)S(1)}) fusion(s32[16,10,4]{2,1,0:T(8,128)S(1)} %slice_convert_fusion, s32[]{:T(128)S(6)} %mul.26), kind=kLoop, calls=%fused_computation.27 | loop fusion | flops 479 | bytes 4488 | tf_op jit(solution)/shard_map/reduce_sum | solution.py:399
  41.3 0.1 add.31
  41.4 0.1 gt.26
  42.2 0.6 reshape_squeeze.16.block_ref
  42.8 0.6 reshape_squeeze.17.start_ref
  43.4 0.6 and_select_fusion.5.row_ref
  44.0 1.6 %collective-permute-start = (bf16[16,176,128]{2,1,0:T(8,128)(2,1)S(1)}, bf16[16,176,128]{2,1,0:T(8,128)(2,1)S(1)}, u32[]{:S(2)}, u32[]{:S(2)}) collective-permute-start(bf16[16,176,128]{2,1,0:T(8,128)(2,1)S(1)} %all-to-all-done.pool_ref), channel_id=1, source_target_pairs={{0,16},{16,0},{1,17},{17,1},{2,18},{18,2},{3,19},{19,3},{4,20},{20... | collective-permute-start | bytes 2162696 | tf_op jit(solution)/shard_map/ppermute | solution.py:391
  45.6 0.5 reshape.98.weight_ref
  46.1 0.0 copy-done
  46.1 8.8 %place_subgrids.1.band_ref = bf16[2,32,128,128]{3,2,1,0:T(8,128)(2,1)} custom-call(s32[160]{0:T(256)} %and_select_fusion.5.row_ref, s32[160]{0:T(256)} %reshape_squeeze.16.block_ref, s32[160]{0:T(256)} %reshape_squeeze.17.start_ref, f32[16]{0:T(128)} %reshape.98.weight_ref, bf16[16,176,128]{2,1,0:T(8,128)(2,1)} %copy-done), custom_call_target="tpu_custom_call" | custom-call | flops 8000000000 | bytes 10000000 | tf_op jit(solution)/shard_map/place_subgrids/pallas_call | solution.py:407
  55.0 7.5 %collective-permute-done.pool_ref = bf16[16,176,128]{2,1,0:T(8,128)(2,1)S(1)} collective-permute-done((bf16[16,176,128]{2,1,0:T(8,128)(2,1)S(1)}, bf16[16,176,128]{2,1,0:T(8,128)(2,1)S(1)}, u32[]{:S(2)}, u32[]{:S(2)}) %collective-permute-start) | collective-permute-done | bytes 720928 | tf_op jit(solution)/shard_map/ppermute | solution.py:391
  62.5 0.0 copy-start.1
  62.5 1.6 %slice_reduce_fusion.5 = (s32[]{:T(128)}, s32[16,10]{1,0:T(8,128)S(1)}, s32[16,10]{1,0:T(8,128)S(1)}, s32[16,10]{1,0:T(8,128)S(1)}) fusion(s32[16,10,4]{2,1,0:T(8,128)S(1)} %slice_convert_fusion.1, s32[]{:T(128)S(6)} %mul.26), kind=kLoop, calls=%fused_computation.28 | loop fusion | flops 479 | bytes 4488 | tf_op jit(solution)/shard_map/reduce_sum | solution.py:399
  64.0 0.4 compare_reduce_fusion.1
  64.4 0.1 add.29
  64.5 0.1 gt.23
  65.3 0.7 reshape_squeeze.14.block_ref
  65.9 0.6 reshape_squeeze.15.start_ref
  66.6 0.6 and_select_fusion.6.row_ref
  67.2 0.6 reshape.97.weight_ref
  67.7 0.0 copy-done.1
  67.7 15.2 %row_sections.1 = (bf16[16,128,256]{2,1,0:T(8,128)(2,1)}, bf16[16,128,256]{2,1,0:T(8,128)(2,1)}) custom-call(s32[160]{0:T(256)} %and_select_fusion.6.row_ref, s32[160]{0:T(256)} %reshape_squeeze.14.block_ref, s32[160]{0:T(256)} %reshape_squeeze.15.start_ref, f32[16]{0:T(128)} %reshape.97.weight_ref, bf16[16,176,128]{2,1,0:T(8,128)(2,1)} %copy-done.1, ...), custom_call_target="tpu_custom_call" | custom-call | tf_op jit(solution)/shard_map/row_sections/pallas_call | solution.py:420
  82.9 0.0 copy-start.3
  82.9 67.5 %columns.1 = (f32[8,256,128]{2,1,0:T(8,128)}, f32[8,256,128]{2,1,0:T(8,128)}) custom-call(bf16[16,128,256]{2,1,0:T(8,128)(2,1)} %get-tuple-element.9.refs_0_, bf16[16,128,256]{2,1,0:T(8,128)(2,1)} %get-tuple-element.10.refs_1_, bf16[16,256,256]{2,1,0:T(8,128)(2,1)} %dynamic-slice_bitcast_fusion.refs_2_), custom_call_target="tpu_custom_call" | custom-call | tf_op jit(solution)/shard_map/columns/pallas_call | solution.py:438
  150.4 0.0 copy-done.3
  150.4 3.2 %fusion = f32[8,256,256]{2,1,0:T(8,128)} fusion(f32[8,256,128]{2,1,0:T(8,128)} %get-tuple-element.12, f32[8,256,128]{2,1,0:T(8,128)} %get-tuple-element.11, f32[256]{0:T(256)S(1)} %copy-done.3, f32[8,256]{1,0:T(8,128)S(1)} %broadcast_multiply_fusion), kind=kLoop, calls=%fused_computation.1 | loop fusion | flops 1572864 | bytes 4203520 | tf_op jit(solution)/shard_map/mul | solution.py:463
  (7 shorter events, 0.1 us)
Async XLA Ops:
  15.5 23.9 %all-to-all-start = ((bf16[16,176,128]{2,1,0:T(8,128)(2,1)}), bf16[16,176,128]{2,1,0:T(8,128)(2,1)S(1)}, u32[]{:S(2)}, u32[]{:S(2)}) async-start(bf16[16,176,128]{2,1,0:T(8,128)(2,1)} %grid_slots.1), calls=%async_computation | async-start | bytes 1441792 | tf_op jit(solution)/shard_map/all_to_all | solution.py:387
  21.7 3.1 %copy-start.2 = (f32[8,256]{1,0:T(8,128)S(1)}, f32[8,256]{1,0:T(8,128)}, u32[]{:S(2)}) copy-start(f32[8,256]{1,0:T(8,128)} %param.16) | copy-start | bytes 24580
  39.4 6.7 %copy-start = (bf16[16,176,128]{2,1,0:T(8,128)(2,1)}, bf16[16,176,128]{2,1,0:T(8,128)(2,1)S(1)}, u32[]{:S(2)}) copy-start(bf16[16,176,128]{2,1,0:T(8,128)(2,1)S(1)} %all-to-all-done.pool_ref) | copy-start | bytes 2162692
  44.0 18.4 %collective-permute-start = (bf16[16,176,128]{2,1,0:T(8,128)(2,1)S(1)}, bf16[16,176,128]{2,1,0:T(8,128)(2,1)S(1)}, u32[]{:S(2)}, u32[]{:S(2)}) collective-permute-start(bf16[16,176,128]{2,1,0:T(8,128)(2,1)S(1)} %all-to-all-done.pool_ref), channel_id=1, source_target_pairs={{0,16},{16,0},{1,17},{17,1},{2,18},{18,2},{3,19},{19,3},{4,20},{20... | collective-permute-start | bytes 2162696 | tf_op jit(solution)/shard_map/ppermute | solution.py:391
  62.5 5.3 %copy-start.1 = (bf16[16,176,128]{2,1,0:T(8,128)(2,1)}, bf16[16,176,128]{2,1,0:T(8,128)(2,1)S(1)}, u32[]{:S(2)}) copy-start(bf16[16,176,128]{2,1,0:T(8,128)(2,1)S(1)} %collective-permute-done.pool_ref) | copy-start | bytes 2162692
  82.9 67.5 %copy-start.3 = (f32[256]{0:T(256)S(1)}, f32[256]{0:T(256)}, u32[]{:S(2)}) copy-start(f32[256]{0:T(256)} %param.17) | copy-start | bytes 3076

commit v3 on v2

--- a/solution.py
+++ b/solution.py
@@ -47,8 +47,26 @@
     return low + high
 
 
-def grid_kernel(pairs, src_ref, data_ref, info_ref, out_ref):
+def grid_kernel(
+    pairs, tile_count, epoch_count, src_ref, data_ref, info_ref, got_ref, others_ref, *scratch
+):
+    packed, t_send, t_recv, x_send, x_recv = scratch
+    me, epoch = lax.axis_index("tile"), lax.axis_index("epoch")
+    mesh_id = pl.DeviceIdType.MESH
     cells = lax.broadcasted_iota(jnp.int32, (SUB, data_ref.shape[2]), 0).astype(jnp.float32)
+
+    barrier = pltpu.get_barrier_semaphore()
+
+    def greet(k, carry):
+        peer = lax.rem(me + k, tile_count)
+        pl.semaphore_signal(barrier, inc=1, device_id={"tile": peer}, device_id_type=mesh_id)
+        return carry
+
+    lax.fori_loop(1, tile_count, greet, 0)
+    for k in range(1, epoch_count):
+        peer = lax.rem(epoch + k, epoch_count)
+        pl.semaphore_signal(barrier, inc=1, device_id={"epoch": peer}, device_id_type=mesh_id)
+    pl.semaphore_wait(barrier, tile_count + epoch_count - 2)
 
     def one(slot):
         data = data_ref[slot]
@@ -62,15 +80,65 @@
             preferred_element_type=jnp.float32,
         )
 
-    def per_tile(tile, carry):
+    def make(tile, out_ref):
         for k in range(pairs):
             at = (tile * pairs + k) * 2
             both = jnp.concatenate([one(src_ref[at]), one(src_ref[at + 1])], 1)
             out_ref[tile, k * SUB : (k + 1) * SUB, :] = both.astype(jnp.bfloat16)
         out_ref[tile, pairs * SUB :, :] = info_ref[tile]
-        return carry
-
-    lax.fori_loop(0, out_ref.shape[0], per_tile, 0)
+
+    def tile_copy(k):
+        peer = lax.rem(me + k, tile_count)
+        return pltpu.make_async_remote_copy(
+            src_ref=packed.at[peer],
+            dst_ref=got_ref.at[me],
+            send_sem=t_send.at[k],
+            recv_sem=t_recv.at[k],
+            device_id={"tile": peer},
+            device_id_type=mesh_id,
+        )
+
+    def epoch_copy(k, j):
+        origin = lax.rem(me + tile_count - k, tile_count)
+        return pltpu.make_async_remote_copy(
+            src_ref=got_ref.at[origin],
+            dst_ref=others_ref.at[(j - 1) * tile_count + origin],
+            send_sem=x_send.at[(j - 1) * tile_count + k],
+            recv_sem=x_recv.at[(j - 1) * tile_count + k],
+            device_id={"epoch": lax.rem(epoch + j, epoch_count)},
+            device_id_type=mesh_id,
+        )
+
+    def send(k, carry):
+        make(lax.rem(me + k, tile_count), packed)
+        tile_copy(k).start()
+        return carry
+
+    make(me, got_ref)
+    for j in range(1, epoch_count):
+        epoch_copy(0, j).start()
+    lax.fori_loop(1, tile_count, send, 0)
+
+    def forward(k, carry):
+        tile_copy(k).wait_recv()
+        for j in range(1, epoch_count):
+            epoch_copy(k, j).start()
+        return carry
+
+    lax.fori_loop(1, tile_count, forward, 0)
+
+    def sent_all(k, carry):
+        tile_copy(k).wait_send()
+        return carry
+
+    lax.fori_loop(1, tile_count, sent_all, 0)
+
+    def crossed(k, carry):
+        for j in range(1, epoch_count):
+            epoch_copy(k, j).wait()
+        return carry
+
+    lax.fori_loop(0, tile_count, crossed, 0)
 
 
 def add_slots(pairs, row_ref, block_ref, start_ref, weight_ref, pool_ref, acc):
@@ -375,21 +443,28 @@
     info = jnp.pad(jnp.stack(fields[:4], -1), ((0, 0), (0, 0), (0, LANES - 4))).astype(jnp.bfloat16)
     data = jnp.concatenate([coords[0], samples[0].astype(jnp.float32)], 1)
 
-    packed = pl.pallas_call(
-        functools.partial(grid_kernel, pairs),
-        out_shape=jax.ShapeDtypeStruct((tile_count, block_rows, LANES), jnp.bfloat16),
+    tile_sems = pltpu.SemaphoreType.DMA((tile_count,))
+    epoch_sems = pltpu.SemaphoreType.DMA(((epoch_count - 1) * tile_count,))
+    got, others = pl.pallas_call(
+        functools.partial(grid_kernel, pairs, tile_count, epoch_count),
+        out_shape=[
+            jax.ShapeDtypeStruct((n * tile_count, block_rows, LANES), jnp.bfloat16)
+            for n in (1, epoch_count - 1)
+        ],
         in_specs=smem(1) + vmem(2),
-        out_specs=vmem(1)[0],
-        compiler_params=params,
+        out_specs=vmem(2),
+        scratch_shapes=[
+            pltpu.VMEM((tile_count, block_rows, LANES), jnp.bfloat16),
+            tile_sems,
+            tile_sems,
+            epoch_sems,
+            epoch_sems,
+        ],
+        compiler_params=pltpu.CompilerParams(
+            vmem_limit_bytes=VMEM_BYTES, collective_id=1, has_side_effects=True
+        ),
         name="grid_slots",
     )(source, data, info)
-
-    got = lax.all_to_all(packed, "tile", split_axis=0, concat_axis=0, tiled=True)
-    others = []
-    for k in range(1, epoch_count):
-        ring = [(e, (e + k) % epoch_count) for e in range(epoch_count)]
-        others.append(lax.ppermute(got, "epoch", ring))
-    others = jnp.concatenate(others, 0) if epoch_count > 2 else others[0]
     spare = rows_here + 2 * SUB
     lane_blocks = tile_count * block_len // LANES
 

time: 154 us -> 152 us (0.987)
  Pallas kernels: 98.1 us -> 124 us
  waiting for transfers between devices: 22 us -> 0 us
  starting transfers between devices: 7.8 us -> 0 us
  other arithmetic: 15.5 us -> 17.3 us
    pallas_call x1, Pallas kernels: 6.59 us -> 29.2 us  [body(): pl.pallas_call(functools.partial(grid_kernel, pairs, tile_count, epoch_co...]
    all_to_all x1 -> x0, waiting for transfers between devices: 14.5 us -> none  [body(): lax.all_to_all(packed, 'tile', split_axis=0, concat_axis=0, tiled=True)]
    ppermute x1 -> x0, waiting for transfers between devices: 7.49 us -> none  [body(): others.append(lax.ppermute(got, 'epoch', ring))]
    all_to_all x1 -> x0, starting transfers between devices: 6.24 us -> none  [body(): lax.all_to_all(packed, 'tile', split_axis=0, concat_axis=0, tiled=True)]
    pallas_call x1, Pallas kernels: 67.5 us -> 70.7 us  [body(): pl.pallas_call(functools.partial(columns_kernel, tile_count, epoch_count,...]
    convert_element_type x2, other arithmetic: 0.03 us -> 1.72 us  [places(): table = pool[:, pairs * SUB:pairs * SUB + capacity, :4].astype(jnp.int32)]
    ppermute x1 -> x0, starting transfers between devices: 1.56 us -> none  [body(): others.append(lax.ppermute(got, 'epoch', ring))]
  transfers between devices with their start and end apart: 2 -> 0, of which waited for: 2 -> 0; matrix products, arithmetic and copies ran while one was open for 2% -> 0% of each run, Pallas kernels for 6% -> 0%
where the time goes in v3:
time: 152 us; the launch traced here: 151 us
  Pallas kernels  124 us (82%)
  other arithmetic  17.3 us (11%)
  local copies, waits for them, and re-layouts  8.55 us (6%)
  between operations  1.56 us (1%)
    pallas_call x1, Pallas kernels, body(): pl.pallas_call(functools.partial(columns_kernel, tile_count, epoch_count,...  70.7 us
    pallas_call x1, Pallas kernels, body(): pl.pallas_call(functools.partial(grid_kernel, pairs, tile_count, epoch_co...  29.2 us
    pallas_call x1, Pallas kernels, body(): pl.pallas_call(functools.partial(rows_kernel, pairs), out_shape=[jax.Shap...  15.2 us
    pallas_call x1, Pallas kernels, body(): pl.pallas_call(functools.partial(place_kernel, pairs), out_shape=jax.Shap...  8.84 us
    mul x1, other arithmetic, body(): image_sum * (image_scale * taper_rows)[:, :, None]  3.21 us
    reduce_sum x2, other arithmetic, places(): counts = jnp.sum(table[:, :, 0].reshape(-1, tile_count * capacity), 1)  3.19 us
    squeeze x1, local copies, waits for them, and re-layouts, body(): lax.dynamic_index_in_dim(jnp.asarray(last), epoch_index, 0, keepdims=False)  3.09 us

profile of v3, /device:TPU:12, one launch (start us, length us, event | category | flops | bytes accessed | tf_op | source)
XLA Modules:
  0.0 151.4 jit_solution(600791290061645399)
XLA Ops:
  0.0 0.9 convert_reduce_fusion
  0.9 0.7 iota_compare_fusion.2
  1.6 0.7 and_select_fusion.8
  2.2 2.1 %fusion.2 = (s32[16,16]{1,0:T(8,128)S(1)}, s32[16,16]{1,0:T(8,128)S(1)}, s32[16,16]{1,0:T(8,128)S(1)}, s32[16,16]{1,0:T(8,128)S(1)}, s32[16,16]{1,0:T(8,128)S(1)}) fusion(pred[16,128]{1,0:T(8,128)(4,1)S(1)} %iota_compare_fusion.1, pred[16,128]{1,0:T(8,128)(4,1)S(1)} %iota_compare_fusion.2, s32[128]{0:T(128)S(1)} %get-tuple-element.31, ...), kind=kLoop, calls=%fused_computation.10 | loop fusion | flops 359168 | bytes 10752 | tf_op jit(solution)/shard_map/reduce_sum | solution.py:433
  4.4 0.2 copy.17
  4.6 0.6 pad.5.info_ref
  5.2 0.7 reshape.96.src_ref
  5.9 1.0 bitcast_convert_fusion
  6.9 2.0 %pad_maximum_fusion.data_ref = f32[128,4,256]{2,1,0:T(4,128)} fusion(f32[128,2,256]{2,1,0:T(2,128)S(1)} %bitcast_convert_fusion, f32[128,2,256]{2,1,0:T(2,128)} %bitcast.32), kind=kLoop, calls=%fused_computation.3 | loop fusion | flops 131072 | bytes 1048576 | tf_op jit(solution)/shard_map/concatenate | solution.py:444
  8.9 29.2 %grid_slots.1 = (bf16[16,176,128]{2,1,0:T(8,128)(2,1)}, bf16[16,176,128]{2,1,0:T(8,128)(2,1)}) custom-call(s32[160]{0:T(256)} %reshape.96.src_ref, f32[128,4,256]{2,1,0:T(4,128)} %pad_maximum_fusion.data_ref, bf16[16,16,128]{2,1,0:T(8,128)(2,1)} %pad.5.info_ref), custom_call_target="tpu_custom_call" | custom-call | tf_op jit(solution)/shard_map/grid_slots/pallas_call | solution.py:448
  38.1 0.9 slice_convert_fusion
  39.0 1.6 %slice_reduce_fusion.4 = (s32[]{:T(128)}, s32[16,10]{1,0:T(8,128)S(1)}, s32[16,10]{1,0:T(8,128)S(1)}, s32[16,10]{1,0:T(8,128)S(1)}) fusion(s32[16,10,4]{2,1,0:T(8,128)S(1)} %slice_convert_fusion, s32[]{:T(128)S(6)} %mul.26), kind=kLoop, calls=%fused_computation.27 | loop fusion | flops 479 | bytes 4488 | tf_op jit(solution)/shard_map/reduce_sum | solution.py:474
  40.5 0.1 add.31
  40.6 0.4 compare_reduce_fusion
  41.0 0.1 gt.26
  41.1 0.6 and_select_fusion.5.row_ref
  42.3 0.5 reshape.98.weight_ref
  42.8 0.7 reshape_squeeze.16.block_ref
  43.5 0.7 reshape_squeeze.17.start_ref
  44.1 8.8 %place_subgrids.1.band_ref = bf16[2,32,128,128]{3,2,1,0:T(8,128)(2,1)} custom-call(s32[160]{0:T(256)} %and_select_fusion.5.row_ref, s32[160]{0:T(256)} %reshape_squeeze.16.block_ref, s32[160]{0:T(256)} %reshape_squeeze.17.start_ref, f32[16]{0:T(128)} %reshape.98.weight_ref, bf16[16,176,128]{2,1,0:T(8,128)(2,1)} %get-tuple-element.12.pool_ref), custom_call_target="tpu_custom_call" | custom-call | flops 8000000000 | bytes 10000000 | tf_op jit(solution)/shard_map/place_subgrids/pallas_call | solution.py:482
  53.0 0.9 slice_convert_fusion.1
  53.8 1.6 %slice_reduce_fusion.5 = (s32[]{:T(128)}, s32[16,10]{1,0:T(8,128)S(1)}, s32[16,10]{1,0:T(8,128)S(1)}, s32[16,10]{1,0:T(8,128)S(1)}) fusion(s32[16,10,4]{2,1,0:T(8,128)S(1)} %slice_convert_fusion.1, s32[]{:T(128)S(6)} %mul.26), kind=kLoop, calls=%fused_computation.28 | loop fusion | flops 479 | bytes 4488 | tf_op jit(solution)/shard_map/reduce_sum | solution.py:474
  55.5 0.1 add.29
  55.6 0.4 compare_reduce_fusion.1
  55.9 0.1 gt.23
  56.0 0.6 and_select_fusion.6.row_ref
  57.4 0.5 reshape.97.weight_ref
  57.9 0.6 reshape_squeeze.14.block_ref
  58.5 0.6 reshape_squeeze.15.start_ref
  59.1 15.2 %row_sections.1 = (bf16[16,128,256]{2,1,0:T(8,128)(2,1)}, bf16[16,128,256]{2,1,0:T(8,128)(2,1)}) custom-call(s32[160]{0:T(256)} %and_select_fusion.6.row_ref, s32[160]{0:T(256)} %reshape_squeeze.14.block_ref, s32[160]{0:T(256)} %reshape_squeeze.15.start_ref, f32[16]{0:T(128)} %reshape.97.weight_ref, bf16[16,176,128]{2,1,0:T(8,128)(2,1)} %get-tuple-element.11.pool_ref, ...), custom_call_target="tpu_custom_call" | custom-call | tf_op jit(solution)/shard_map/row_sections/pallas_call | solution.py:495
  74.3 3.1 %dynamic-slice_bitcast_fusion.refs_2_ = bf16[16,256,256]{2,1,0:T(8,128)(2,1)} fusion(bf16[2,16,256,256]{3,2,1,0:T(8,128)(2,1)} %constant.70.clone, s32[]{:T(128)S(6)} %select_n.50), kind=kLoop, calls=%fused_computation.2 | loop fusion | bytes 4194308 | tf_op jit(solution)/shard_map/jit(dynamic_index_in_dim)/squeeze | solution.py:508
  77.4 0.0 copy-start
  77.4 0.0 copy-start.1
  77.4 70.7 %columns.1 = (f32[8,256,128]{2,1,0:T(8,128)}, f32[8,256,128]{2,1,0:T(8,128)}) custom-call(bf16[16,128,256]{2,1,0:T(8,128)(2,1)} %get-tuple-element.13.refs_0_, bf16[16,128,256]{2,1,0:T(8,128)(2,1)} %get-tuple-element.14.refs_1_, bf16[16,256,256]{2,1,0:T(8,128)(2,1)} %dynamic-slice_bitcast_fusion.refs_2_), custom_call_target="tpu_custom_call" | custom-call | tf_op jit(solution)/shard_map/columns/pallas_call | solution.py:513
  148.2 0.0 copy-done
  148.2 0.0 copy-done.1
  148.2 3.2 %fusion = f32[8,256,256]{2,1,0:T(8,128)} fusion(f32[8,256,128]{2,1,0:T(8,128)} %get-tuple-element.16, f32[8,256,128]{2,1,0:T(8,128)} %get-tuple-element.15, f32[256]{0:T(256)S(1)} %copy-done.1, f32[8,256]{1,0:T(8,128)S(1)} %broadcast_multiply_fusion), kind=kLoop, calls=%fused_computation.1 | loop fusion | flops 1572864 | bytes 4203520 | tf_op jit(solution)/shard_map/mul | solution.py:538
  (5 shorter events, 0.0 us)
Async XLA Ops:
  77.4 70.8 %copy-start = (f32[8,256]{1,0:T(8,128)S(1)}, f32[8,256]{1,0:T(8,128)}, u32[]{:S(2)}) copy-start(f32[8,256]{1,0:T(8,128)} %param.16) | copy-start | bytes 24580
  77.4 70.8 %copy-start.1 = (f32[256]{0:T(256)S(1)}, f32[256]{0:T(256)}, u32[]{:S(2)}) copy-start(f32[256]{0:T(256)} %param.17) | copy-start | bytes 3076
